TPU v7x, 32 devices: a whole 2x2x4 slice. The times are simulated.
32 devices in a mesh: dp: 4 (over y, core), fsdp: 8 (over z, x).
Axes of the slice: x: 2, y: 2, z: 4, core: 2. Of those that a mesh axis runs over, the one named last changes fastest.
Arguments:
- tokens: bfloat16 [32, 1024, 1024], P(('dp', 'fsdp')), may hold values from -6 to 6
- doc_ids: int32 [32, 1024], P(('dp', 'fsdp')), may hold values from 0 to 7, never falling along the last dimension, each value on 1 to 512 neighbouring positions
- norm_gain: bfloat16 [1024], P(('dp', 'fsdp')), may hold values from 0.25 to 1.75
- w_query_heads: bfloat16 [1024, 96], P(('dp', 'fsdp')), may hold values from -0.625 to 0.625
- w_query_dims: bfloat16 [1024, 384], P(('dp', 'fsdp')), may hold values from -0.1875 to 0.1875
- w_key_heads: bfloat16 [1024, 32], P(('dp', 'fsdp')), may hold values from -0.375 to 0.375
- w_key_dims: bfloat16 [1024, 128], P(('dp', 'fsdp')), may hold values from -0.1875 to 0.1875
- w_value_heads: bfloat16 [1024, 32], P(('dp', 'fsdp')), may hold values from -0.1875 to 0.1875
- w_value_dims: bfloat16 [1024, 128], P(('dp', 'fsdp')), may hold values from -0.1875 to 0.1875
- w_output: bfloat16 [1024, 1024], P(('dp', 'fsdp')), may hold values from -1.5 to 1.5
- mlp_gain: bfloat16 [1024], P(('dp', 'fsdp')), may hold values from 0.25 to 1.75
- w_gate: bfloat16 [1024, 2816], P(('dp', 'fsdp')), may hold values from -0.1875 to 0.1875
- w_up: bfloat16 [1024, 2816], P(('dp', 'fsdp')), may hold values from -0.1875 to 0.1875
- w_down: bfloat16 [2816, 1024], P(('dp', 'fsdp')), may hold values from -0.109375 to 0.109375
- out_grad: bfloat16 [32, 1024, 1024], P(('dp', 'fsdp')), may hold values from -6 to 6
Outputs:
- output: bfloat16 [32, 1024, 1024], P(('dp', 'fsdp'))
- grad_tokens: bfloat16 [32, 1024, 1024], P(('dp', 'fsdp'))
- grad_norm_gain: float32 [1024], P(('dp', 'fsdp'))
- grad_w_query_heads: float32 [1024, 96], P(('dp', 'fsdp'))
- grad_w_query_dims: float32 [1024, 384], P(('dp', 'fsdp'))
- grad_w_key_heads: float32 [1024, 32], P(('dp', 'fsdp'))
- grad_w_key_dims: float32 [1024, 128], P(('dp', 'fsdp'))
- grad_w_value_heads: float32 [1024, 32], P(('dp', 'fsdp'))
- grad_w_value_dims: float32 [1024, 128], P(('dp', 'fsdp'))
- grad_w_output: float32 [1024, 1024], P(('dp', 'fsdp'))
- grad_mlp_gain: float32 [1024], P(('dp', 'fsdp'))
- grad_w_gate: float32 [1024, 2816], P(('dp', 'fsdp'))
- grad_w_up: float32 [1024, 2816], P(('dp', 'fsdp'))
- grad_w_down: float32 [2816, 1024], P(('dp', 'fsdp'))
Inputs may be any that keep to these rules, and one draw needn't show every extreme that they name: `doc_ids`: along each row the document numbers never fall; a document holds at most 512 tokens.
All inputs are finite; a program needn't handle non-finite values.
Results may differ from a plain program's by a relative error of at most 0.015.
The roundings to bfloat16 on the way count: a program that leaves them out, or rounds other values in their place, can miss the bound.
Values may be sent and summed in bfloat16 or wider, within the bound.
A program may use at most 320 MiB of HBM per device.

v0:
```python
import math

import jax
import jax.numpy as jnp
from jax import lax
from jax.sharding import PartitionSpec as P

D = 1024
H = 16
DH = 64
RQ = 6
RK = 2


epsilon = 1e-06
theta_base = 10000.0
highest = lax.Precision.HIGHEST


def rotary_tables(seq_len, half_dim):
    position = jnp.arange(seq_len, dtype=jnp.float32)
    inverse = jnp.exp(
        -math.log(theta_base) * 2.0 * jnp.arange(half_dim, dtype=jnp.float32) / (2.0 * half_dim)
    )
    angle = position[:, None] * inverse[None, :]
    return (jnp.cos(angle), jnp.sin(angle))


def rotate(factor, cosine_table, sine_table):
    half_dim = factor.shape[-1] // 2
    first_half = factor[..., :half_dim]
    second_half = factor[..., half_dim:]
    cosine_part = cosine_table[:, None, :]
    sine_part = sine_table[:, None, :]
    return jnp.concatenate(
        [
            first_half * cosine_part - second_half * sine_part,
            first_half * sine_part + second_half * cosine_part,
        ],
        axis=-1,
    )


def rotate_back(grad_factor, cosine_table, sine_table):
    half_dim = grad_factor.shape[-1] // 2
    first_half = grad_factor[..., :half_dim]
    second_half = grad_factor[..., half_dim:]
    cosine_part = cosine_table[:, None, :]
    sine_part = sine_table[:, None, :]
    return jnp.concatenate(
        [
            first_half * cosine_part + second_half * sine_part,
            second_half * cosine_part - first_half * sine_part,
        ],
        axis=-1,
    )


def rms_scale(values):
    return lax.rsqrt(jnp.mean(values * values, axis=-1, keepdims=True) + epsilon)


def forward_dot(left, right):
    return jnp.dot(left, right, preferred_element_type=jnp.float32)


def outer_sum(left, right):
    return lax.dot_general(
        left, right, (((0,), (0,)), ((), ())), preferred_element_type=jnp.float32
    )


def back_dot(grad_rows, weight):
    return lax.dot_general(
        grad_rows, weight, (((1,), (1,)), ((), ())), preferred_element_type=jnp.float32
    )


def combine_factors(heads_act, dims_act, rank_count):
    return jnp.einsum("bsrh,bsrd->bshd", heads_act, dims_act, precision=highest) / rank_count


def split_factors(grad_full, heads_act, dims_act, rank_count):
    grad_heads = jnp.einsum("bshd,bsrd->bsrh", grad_full, dims_act, precision=highest) / rank_count
    grad_dims = jnp.einsum("bshd,bsrh->bsrd", grad_full, heads_act, precision=highest) / rank_count
    return (grad_heads, grad_dims)


def on_device(
    tokens,
    doc_ids,
    norm_gain,
    w_query_heads,
    w_query_dims,
    w_key_heads,
    w_key_dims,
    w_value_heads,
    w_value_dims,
    w_output,
    mlp_gain,
    w_gate,
    w_up,
    w_down,
    out_grad,
):
    row_count = tokens.shape[0]
    seq_len = tokens.shape[1]
    token_count = row_count * seq_len
    score_scale = 1.0 / math.sqrt(DH)
    cosine_table, sine_table = rotary_tables(seq_len, DH // 2)
    block_len = min(512, seq_len)
    block_count = seq_len // block_len
    positions = jnp.arange(seq_len, dtype=jnp.int32)
    starts = jnp.arange(block_count) * block_len
    attn_full = (
        lax.all_gather(norm_gain, ("dp", "fsdp"), axis=0, tiled=True),
        lax.all_gather(w_query_heads, ("dp", "fsdp"), axis=0, tiled=True),
        lax.all_gather(w_query_dims, ("dp", "fsdp"), axis=0, tiled=True),
        lax.all_gather(w_key_heads, ("dp", "fsdp"), axis=0, tiled=True),
        lax.all_gather(w_key_dims, ("dp", "fsdp"), axis=0, tiled=True),
        lax.all_gather(w_value_heads, ("dp", "fsdp"), axis=0, tiled=True),
        lax.all_gather(w_value_dims, ("dp", "fsdp"), axis=0, tiled=True),
        lax.all_gather(w_output, ("dp", "fsdp"), axis=0, tiled=True),
    )
    (
        gain_one,
        query_heads_w,
        query_dims_w,
        key_heads_w,
        key_dims_w,
        value_heads_w,
        value_dims_w,
        output_w,
    ) = attn_full
    inputs_flat = tokens.astype(jnp.float32).reshape(token_count, D)
    scale_one = rms_scale(inputs_flat)
    normed = (inputs_flat * scale_one * gain_one.astype(jnp.float32)).astype(jnp.bfloat16)
    heads_query = forward_dot(normed, query_heads_w).reshape(row_count, seq_len, RQ, H)
    dims_query = rotate(
        forward_dot(normed, query_dims_w).reshape(row_count, seq_len, RQ, DH),
        cosine_table,
        sine_table,
    )
    heads_key = forward_dot(normed, key_heads_w).reshape(row_count, seq_len, RK, H)
    dims_key = rotate(
        forward_dot(normed, key_dims_w).reshape(row_count, seq_len, RK, DH),
        cosine_table,
        sine_table,
    )
    heads_value = forward_dot(normed, value_heads_w).reshape(row_count, seq_len, RK, H)
    dims_value = forward_dot(normed, value_dims_w).reshape(row_count, seq_len, RK, DH)
    query_full = combine_factors(heads_query, dims_query, RQ).astype(jnp.bfloat16)
    key_full = combine_factors(heads_key, dims_key, RK).astype(jnp.bfloat16)
    value_full = combine_factors(heads_value, dims_value, RK).astype(jnp.bfloat16)

    def block_scores(block_start):
        query_block = lax.dynamic_slice_in_dim(query_full, block_start, block_len, 1)
        query_doc = lax.dynamic_slice_in_dim(doc_ids, block_start, block_len, 1)
        scores = (
            jnp.einsum("bqhd,bkhd->bhqk", query_block, key_full, preferred_element_type=jnp.float32)
            * score_scale
        )
        query_pos = block_start + jnp.arange(block_len, dtype=jnp.int32)
        allowed = (positions[None, None, :] <= query_pos[None, :, None]) & (
            query_doc[:, :, None] == doc_ids[:, None, :]
        )
        return (jnp.where(allowed[:, None, :, :], scores, -1e30), query_block)

    def forward_block(block_start):
        masked, query_block = block_scores(block_start)
        row_max = jnp.max(masked, axis=-1, keepdims=True)
        exp_terms = jnp.exp(masked - row_max)
        row_total = jnp.sum(exp_terms, axis=-1, keepdims=True)
        attn_probs = (exp_terms / row_total).astype(jnp.bfloat16)
        mixed_block = jnp.einsum(
            "bhqk,bkhd->bqhd", attn_probs, value_full, preferred_element_type=jnp.float32
        )
        return (mixed_block.astype(jnp.bfloat16), (row_max + jnp.log(row_total))[..., 0])

    mixed_blocks, lse_blocks = lax.map(forward_block, starts)
    mixed_heads = jnp.moveaxis(mixed_blocks, 0, 1).reshape(token_count, H * DH)
    middle = inputs_flat + forward_dot(mixed_heads, output_w)
    mlp_full = (
        lax.all_gather(mlp_gain, ("dp", "fsdp"), axis=0, tiled=True),
        lax.all_gather(w_gate, ("dp", "fsdp"), axis=0, tiled=True),
        lax.all_gather(w_up, ("dp", "fsdp"), axis=0, tiled=True),
        lax.all_gather(w_down, ("dp", "fsdp"), axis=0, tiled=True),
    )
    gain_two, gate_w, up_w, down_w = mlp_full
    scale_two = rms_scale(middle)
    gain_two_f = gain_two.astype(jnp.float32)
    normed_two = (middle * scale_two * gain_two_f).astype(jnp.bfloat16)
    gate_proj = forward_dot(normed_two, gate_w)
    up_proj = forward_dot(normed_two, up_w)
    sigmoid_gate = jax.nn.sigmoid(gate_proj)
    silu_gate = gate_proj * sigmoid_gate
    inner_act = (silu_gate * up_proj).astype(jnp.bfloat16)
    result = middle + forward_dot(inner_act, down_w)
    output = result.astype(jnp.bfloat16).reshape(tokens.shape)
    mlp_back = (
        lax.all_gather(mlp_gain, ("dp", "fsdp"), axis=0, tiled=True),
        lax.all_gather(w_gate, ("dp", "fsdp"), axis=0, tiled=True),
        lax.all_gather(w_up, ("dp", "fsdp"), axis=0, tiled=True),
        lax.all_gather(w_down, ("dp", "fsdp"), axis=0, tiled=True),
    )
    attn_back = (
        lax.all_gather(norm_gain, ("dp", "fsdp"), axis=0, tiled=True),
        lax.all_gather(w_query_heads, ("dp", "fsdp"), axis=0, tiled=True),
        lax.all_gather(w_query_dims, ("dp", "fsdp"), axis=0, tiled=True),
        lax.all_gather(w_key_heads, ("dp", "fsdp"), axis=0, tiled=True),
        lax.all_gather(w_key_dims, ("dp", "fsdp"), axis=0, tiled=True),
        lax.all_gather(w_value_heads, ("dp", "fsdp"), axis=0, tiled=True),
        lax.all_gather(w_value_dims, ("dp", "fsdp"), axis=0, tiled=True),
        lax.all_gather(w_output, ("dp", "fsdp"), axis=0, tiled=True),
    )
    gain_two_b, gate_wb, up_wb, down_wb = mlp_back
    (
        gain_one_b,
        query_heads_wb,
        query_dims_wb,
        key_heads_wb,
        key_dims_wb,
        value_heads_wb,
        value_dims_wb,
        output_wb,
    ) = attn_back
    cotangent = out_grad.reshape(token_count, D)
    grad_inner = back_dot(cotangent, down_wb)
    grad_gate = (
        grad_inner * up_proj * sigmoid_gate * (1.0 + gate_proj * (1.0 - sigmoid_gate))
    ).astype(jnp.bfloat16)
    grad_up = (grad_inner * silu_gate).astype(jnp.bfloat16)
    grad_normed_two = back_dot(grad_gate, gate_wb) + back_dot(grad_up, up_wb)
    gained_two = grad_normed_two * gain_two_b.astype(jnp.float32)
    grad_mlp_gain = jnp.sum(grad_normed_two * middle * scale_two, axis=0)
    grad_middle = (
        cotangent.astype(jnp.float32)
        + scale_two * gained_two
        - middle * scale_two**3 * jnp.mean(gained_two * middle, axis=-1, keepdims=True)
    )
    normed_cols = normed_two
    mlp_grads = lax.psum_scatter(
        (grad_mlp_gain, outer_sum(normed_cols, grad_gate), outer_sum(normed_cols, grad_up)),
        ("dp", "fsdp"),
        scatter_dimension=0,
        tiled=True,
    )
    down_grad = lax.psum_scatter(
        outer_sum(inner_act, cotangent), ("dp", "fsdp"), scatter_dimension=0, tiled=True
    )
    grad_branch = grad_middle.astype(jnp.bfloat16)
    grad_mixed = (
        back_dot(grad_branch, output_wb).astype(jnp.bfloat16).reshape(row_count, seq_len, H, DH)
    )

    def backward_block(carry_grads, block_inputs):
        grad_key_sum, grad_value_sum = carry_grads
        block_start, lse_block = block_inputs
        masked, query_block = block_scores(block_start)
        probs = jnp.exp(masked - lse_block[..., None])
        grad_mixed_block = lax.dynamic_slice_in_dim(grad_mixed, block_start, block_len, 1)
        grad_probs = jnp.einsum(
            "bqhd,bkhd->bhqk", grad_mixed_block, value_full, preferred_element_type=jnp.float32
        )
        grad_value_sum = grad_value_sum + jnp.einsum(
            "bhqk,bqhd->bkhd",
            probs.astype(jnp.bfloat16),
            grad_mixed_block,
            preferred_element_type=jnp.float32,
        )
        row_delta = jnp.sum(probs * grad_probs, axis=-1, keepdims=True)
        grad_scores = (probs * (grad_probs - row_delta)).astype(jnp.bfloat16)
        grad_query_block = (
            jnp.einsum("bhqk,bkhd->bqhd", grad_scores, key_full, preferred_element_type=jnp.float32)
            * score_scale
        )
        grad_key_sum = (
            grad_key_sum
            + jnp.einsum(
                "bhqk,bqhd->bkhd", grad_scores, query_block, preferred_element_type=jnp.float32
            )
            * score_scale
        )
        return ((grad_key_sum, grad_value_sum), grad_query_block)

    zeros_full = jnp.zeros((row_count, seq_len, H, DH), jnp.float32)
    (grad_key, grad_value), grad_query_blocks = lax.scan(
        backward_block, (zeros_full, zeros_full), (starts, lse_blocks)
    )
    grad_query = jnp.moveaxis(grad_query_blocks, 0, 1).reshape(row_count, seq_len, H, DH)
    grad_heads_query, grad_dims_query = split_factors(grad_query, heads_query, dims_query, RQ)
    grad_heads_key, grad_dims_key = split_factors(grad_key, heads_key, dims_key, RK)
    grad_heads_value, grad_dims_value = split_factors(grad_value, heads_value, dims_value, RK)
    grad_dims_query = rotate_back(grad_dims_query, cosine_table, sine_table)
    grad_dims_key = rotate_back(grad_dims_key, cosine_table, sine_table)
    factor_pairs = (
        (grad_heads_query, query_heads_wb),
        (grad_dims_query, query_dims_wb),
        (grad_heads_key, key_heads_wb),
        (grad_dims_key, key_dims_wb),
        (grad_heads_value, value_heads_wb),
        (grad_dims_value, value_dims_wb),
    )
    grad_flats = []
    grad_normed = jnp.zeros((token_count, D), jnp.float32)
    for grad_factor, weight in factor_pairs:
        grad_flat = grad_factor.reshape(token_count, weight.shape[1]).astype(jnp.bfloat16)
        grad_flats.append(grad_flat)
        grad_normed = grad_normed + back_dot(grad_flat, weight)
    gained_one = grad_normed * gain_one_b.astype(jnp.float32)
    grad_norm_gain = jnp.sum(grad_normed * inputs_flat * scale_one, axis=0)
    grad_inputs = (
        grad_middle
        + scale_one * gained_one
        - inputs_flat * scale_one**3 * jnp.mean(gained_one * inputs_flat, axis=-1, keepdims=True)
    )
    grad_tokens = grad_inputs.astype(jnp.bfloat16).reshape(tokens.shape)
    normed_cols = normed
    attn_grads = lax.psum_scatter(
        (
            grad_norm_gain,
            outer_sum(normed_cols, grad_flats[0]),
            outer_sum(normed_cols, grad_flats[1]),
            outer_sum(normed_cols, grad_flats[2]),
            outer_sum(normed_cols, grad_flats[3]),
            outer_sum(normed_cols, grad_flats[4]),
            outer_sum(normed_cols, grad_flats[5]),
            outer_sum(mixed_heads, grad_branch),
        ),
        ("dp", "fsdp"),
        scatter_dimension=0,
        tiled=True,
    )
    return (
        output,
        grad_tokens,
        attn_grads[0],
        attn_grads[1],
        attn_grads[2],
        attn_grads[3],
        attn_grads[4],
        attn_grads[5],
        attn_grads[6],
        attn_grads[7],
        mlp_grads[0],
        mlp_grads[1],
        mlp_grads[2],
        down_grad,
    )


def solution(mesh):
    return jax.shard_map(
        on_device,
        mesh=mesh,
        in_specs=(
            P(("dp", "fsdp"), None, None),
            P(("dp", "fsdp"), None),
            P(("dp", "fsdp")),
            P(("dp", "fsdp"), None),
            P(("dp", "fsdp"), None),
            P(("dp", "fsdp"), None),
            P(("dp", "fsdp"), None),
            P(("dp", "fsdp"), None),
            P(("dp", "fsdp"), None),
            P(("dp", "fsdp"), None),
            P(("dp", "fsdp")),
            P(("dp", "fsdp"), None),
            P(("dp", "fsdp"), None),
            P(("dp", "fsdp"), None),
            P(("dp", "fsdp"), None, None),
        ),
        out_specs=(
            P(("dp", "fsdp"), None, None),
            P(("dp", "fsdp"), None, None),
            P(("dp", "fsdp")),
            P(("dp", "fsdp"), None),
            P(("dp", "fsdp"), None),
            P(("dp", "fsdp"), None),
            P(("dp", "fsdp"), None),
            P(("dp", "fsdp"), None),
            P(("dp", "fsdp"), None),
            P(("dp", "fsdp"), None),
            P(("dp", "fsdp")),
            P(("dp", "fsdp"), None),
            P(("dp", "fsdp"), None),
            P(("dp", "fsdp"), None),
        ),
        check_vma=False,
    )
```

profile of v0, /device:TPU:0, one launch (start us, length us, event | category | flops | bytes accessed | tf_op | source)
XLA Modules:
  0.0 2745.2 jit_solution(7048219183550699967)
XLA Ops:
  10.1 72.2 %all_gather.49 = bf16[1024,96]{1,0:T(8,128)(2,1)S(1)} all-gather(bf16[32,96]{1,0:T(8,128)(2,1)} %param.22), channel_id=1, replica_groups=mesh['dp'=4,'fsdp'=8] {'dp','fsdp'}, dimensions={0}, use_global_device_ids=true | all-gather | bytes 202752 | tf_op jit(solution)/shard_map/all_gather | solution.py:117
  86.5 37.5 %all-reduce.5 = (bf16[1024]{0:T(1024)(128)(2,1)S(1)}, bf16[1024]{0:T(1024)(128)(2,1)}) all-reduce(bf16[1024]{0:T(1024)(128)(2,1)S(1)} %dynamic-update-slice, bf16[1024]{0:T(1024)(128)(2,1)S(1)} %dynamic-update-slice.1), channel_id=1, replica_groups=mesh['dp'=4,'fsdp'=8] {'dp','fsdp'}, use_global_device_ids=true, to_apply=%add | all-reduce | flops 2048 | bytes 8192
  128.4 73.5 %all_gather.50 = bf16[1024,384]{1,0:T(8,128)(2,1)S(1)} all-gather(bf16[32,384]{1,0:T(8,128)(2,1)S(1)} %copy-done.50), channel_id=1, replica_groups=mesh['dp'=4,'fsdp'=8] {'dp','fsdp'}, dimensions={0}, use_global_device_ids=true | all-gather | bytes 811008 | tf_op jit(solution)/shard_map/all_gather | solution.py:118
  211.2 16.5 fusion.69
  233.1 66.2 %all_gather.51 = bf16[1024,32]{1,0:T(8,128)(2,1)S(1)} all-gather(bf16[32,32]{1,0:T(8,128)(2,1)S(1)} %copy-done.52), channel_id=1, replica_groups=mesh['dp'=4,'fsdp'=8] {'dp','fsdp'}, dimensions={0}, use_global_device_ids=true | all-gather | bytes 67584 | tf_op jit(solution)/shard_map/all_gather | solution.py:119
  302.7 72.0 %all_gather.52 = bf16[1024,128]{1,0:T(8,128)(2,1)} all-gather(bf16[32,128]{1,0:T(8,128)(2,1)S(1)} %copy-done.53), channel_id=1, replica_groups=mesh['dp'=4,'fsdp'=8] {'dp','fsdp'}, dimensions={0}, use_global_device_ids=true | all-gather | bytes 270336 | tf_op jit(solution)/shard_map/all_gather | solution.py:120
  380.0 14.8 fusion.70
  399.3 64.8 %all_gather.53 = bf16[1024,32]{1,0:T(8,128)(2,1)S(1)} all-gather(bf16[32,32]{1,0:T(8,128)(2,1)S(1)} %copy-done.54), channel_id=1, replica_groups=mesh['dp'=4,'fsdp'=8] {'dp','fsdp'}, dimensions={0}, use_global_device_ids=true | all-gather | bytes 67584 | tf_op jit(solution)/shard_map/all_gather | solution.py:121
  467.5 67.3 %all_gather.54 = bf16[1024,128]{1,0:T(8,128)(2,1)S(1)} all-gather(bf16[32,128]{1,0:T(8,128)(2,1)S(1)} %copy-done.55), channel_id=1, replica_groups=mesh['dp'=4,'fsdp'=8] {'dp','fsdp'}, dimensions={0}, use_global_device_ids=true | all-gather | bytes 270336 | tf_op jit(solution)/shard_map/all_gather | solution.py:122
  540.9 15.8 fusion.71
  562.3 102.7 %while.28 = (s32[]{:T(128)}, bf16[2,1,512,16,64]{2,4,3,1,0:T(8,128)(2,1)}, f32[2,1,16,512]{3,2,1,0:T(8,128)S(1)}, s32[2]{0:T(128)S(1)}, s32[1,1024]{1,0:T(1,128)...) while((s32[]{:T(128)}, ...), condition=%wide.region_4.5_spmd.clone, body=%wide.region_1.4_spmd.clone.sunk | while | flops 2250236416 | bytes 134494480 | solution.py:180
  566.2 16.3 fusion.222
  582.5 15.3 fusion.223
  597.8 14.6 fusion.224
  617.6 16.2 fusion.222
  633.7 15.3 fusion.223
  649.1 14.6 fusion.224
  684.2 11.8 fusion.125
  696.1 11.9 fusion.126
  708.0 22.0 multiply_convert_fusion.1
  755.8 229.9 %while.29 = (s32[]{:T(128)}, f32[1,1024,16,64]{1,3,2,0:T(8,128)}, f32[1,1024,16,64]{1,3,2,0:T(8,128)}, f32[2,1,512,16,64]{2,4,3,1,0:T(8,128)}, s32[2]{0:T(128)S(...) while((s32[]{:T(128)}, f32[1,1024,16,64]{1,3,2,0:T(8,128)}, ...), condition=%wide.region_9.10_spmd.clone, body=%wide.region_7.9_spmd.clone.sunk | while | flops 5501870592 | bytes 300136704 | solution.py:287
  758.6 17.1 fusion.233
  776.9 25.6 multiply_reduce_fusion.5
  802.5 27.8 %multiply_convert_fusion.13 = bf16[16,512,1024]{2,1,0:T(8,128)(2,1)} fusion(f32[16,512,1024]{2,1,0:T(8,128)} %get-tuple-element.512, f32[16,512,1024]{2,1,0:T(8,128)} %fusion.233, f32[16,512]{1,0:T(8,128)S(1)} %get-tuple-element.513, f32[16,512]{1,0:T(8,128)S(1)} %dynamic-slice_bitcast_fusion.2, pred[512,1024]{1,0:T(8,128)(4,1)S(1)} %fusion.234), kind=kLoop, calls=%fused_computation.24.clone.1 | loop fusion | flops 50331648 | bytes 84475904 | tf_op jit(solution)/shard_map/while/body/eval_jaxpr/convert_element_type | solution.py:272
  841.6 17.9 bitcast_add_fusion.5
  872.2 17.0 fusion.233
  890.5 25.6 multiply_reduce_fusion.5
  916.0 27.8 %multiply_convert_fusion.13 = bf16[16,512,1024]{2,1,0:T(8,128)(2,1)} fusion(f32[16,512,1024]{2,1,0:T(8,128)} %get-tuple-element.512, f32[16,512,1024]{2,1,0:T(8,128)} %fusion.233, f32[16,512]{1,0:T(8,128)S(1)} %get-tuple-element.513, f32[16,512]{1,0:T(8,128)S(1)} %dynamic-slice_bitcast_fusion.2, pred[512,1024]{1,0:T(8,128)(4,1)S(1)} %fusion.234), kind=kLoop, calls=%fused_computation.24.clone.1 | loop fusion | flops 50331648 | bytes 84475904 | tf_op jit(solution)/shard_map/while/body/eval_jaxpr/convert_element_type | solution.py:272
  943.8 12.4 bitcast_add_fusion.4
  956.2 19.0 bitcast_add_fusion.5
  1003.8 13.4 fusion.132
  1036.0 13.4 fusion.130
  1058.4 17.9 fusion.128
  1089.3 12.0 fusion.129
  1119.0 11.8 fusion.134
  1130.9 11.8 fusion.135
  1142.8 12.2 fusion.74
  1155.0 11.5 fusion.72
  1190.0 37.1 %all-reduce.4 = (f32[1024]{0:T(1024)S(1)}, f32[1024]{0:T(1024)S(1)}) all-reduce(f32[1024]{0:T(1024)S(1)} %get-tuple-element.321, f32[1024]{0:T(1024)S(1)} %copy-done.56), channel_id=2, replica_groups=mesh['dp'=4,'fsdp'=8] {'dp','fsdp'}, use_global_device_ids=true, to_apply=%region_12.13.clone | all-reduce | flops 2048 | bytes 16384
  1228.3 113.2 %reduce-scatter.19.cloned.1.call-done = f32[32,32]{1,0:T(8,128)} async-done(((f32[1024,32]{1,0:T(8,128)}), f32[32,32]{1,0:T(8,128)}) %reduce-scatter.19.cloned.1.call-update) | async-done | bytes 4112 | tf_op jit(solution)/shard_map/reduce_scatter | solution.py:319
  1341.5 133.1 %reduce-scatter.11.cloned.1.call-done = f32[32,96]{1,0:T(8,128)} async-done(((f32[1024,96]{1,0:T(8,128)}), f32[32,96]{1,0:T(8,128)}) %reduce-scatter.11.cloned.1.call-update) | async-done | bytes 12304 | tf_op jit(solution)/shard_map/reduce_scatter | solution.py:319
  1474.5 133.1 %reduce-scatter.17.cloned.1.call-done = f32[32,128]{1,0:T(8,128)} async-done(((f32[1024,128]{1,0:T(8,128)}), f32[32,128]{1,0:T(8,128)}) %reduce-scatter.17.cloned.1.call-update) | async-done | bytes 16400 | tf_op jit(solution)/shard_map/reduce_scatter | solution.py:319
  1607.6 133.0 %reduce-scatter.21.cloned.1.call-done = f32[32,128]{1,0:T(8,128)} async-done(((f32[1024,128]{1,0:T(8,128)}), f32[32,128]{1,0:T(8,128)}) %reduce-scatter.21.cloned.1.call-update) | async-done | bytes 16400 | tf_op jit(solution)/shard_map/reduce_scatter | solution.py:319
  1740.7 99.9 %reduce-scatter.13.cloned.1.call-done = f32[32,384]{1,0:T(8,128)} async-done(((f32[1024,384]{1,0:T(8,128)}), f32[32,384]{1,0:T(8,128)}) %reduce-scatter.13.cloned.1.call-update) | async-done | bytes 49168 | tf_op jit(solution)/shard_map/reduce_scatter | solution.py:319
  1840.6 145.7 %reduce-scatter.23.cloned.1.call-done = f32[32,1024]{1,0:T(8,128)} async-done(((f32[1024,1024]{1,0:T(8,128)}), f32[32,1024]{1,0:T(8,128)}) %reduce-scatter.23.cloned.1.call-update) | async-done | bytes 131088 | tf_op jit(solution)/shard_map/reduce_scatter | solution.py:319
  1986.3 249.5 %reduce-scatter.25.cloned.1.call-done = f32[32,2816]{1,0:T(8,128)} async-done(((f32[1024,2816]{1,0:T(8,128)}), f32[32,2816]{1,0:T(8,128)}) %reduce-scatter.25.cloned.1.call-update) | async-done | bytes 360464 | tf_op jit(solution)/shard_map/reduce_scatter | solution.py:242
  2235.8 251.4 %reduce-scatter.27.cloned.1.call-done = f32[32,2816]{1,0:T(8,128)} async-done(((f32[1024,2816]{1,0:T(8,128)}), f32[32,2816]{1,0:T(8,128)}) %reduce-scatter.27.cloned.1.call-update) | async-done | bytes 360464 | tf_op jit(solution)/shard_map/reduce_scatter | solution.py:242
  2487.2 251.2 %reduce-scatter.29.cloned.1.call-done = f32[88,1024]{1,0:T(8,128)} async-done(((f32[2816,1024]{1,0:T(8,128)}), f32[88,1024]{1,0:T(8,128)}) %reduce-scatter.29.cloned.1.call-update) | async-done | bytes 360464 | tf_op jit(solution)/shard_map/reduce_scatter | solution.py:248
  (285 shorter events, 241.6 us)
Async XLA Ops:
  7.2 78.9 %copy-start.60 = (bf16[32]{0:T(256)(128)(2,1)S(1)}, bf16[32]{0:T(256)(128)(2,1)}, u32[]{:S(2)}) copy-start(bf16[32]{0:T(256)(128)(2,1)} %param.21) | copy-start | bytes 196
  7.2 79.1 %copy-start.61 = (bf16[32]{0:T(256)(128)(2,1)S(1)}, bf16[32]{0:T(256)(128)(2,1)}, u32[]{:S(2)}) copy-start(bf16[32]{0:T(256)(128)(2,1)} %param.29) | copy-start | bytes 196
  7.2 667.7 %all-gather.5.cloned.1.call-start = ((), (), s32[]{:S(2)}) async-start(), calls=%async_computation.10 | async-start | bytes 2162688 | tf_op jit(solution)/shard_map/all_gather | solution.py:123
  7.9 676.3 %all-gather.7.cloned.1.call-start = ((), (), s32[]{:S(2)}) async-start(), calls=%async_computation.11 | async-start | bytes 5947392 | tf_op jit(solution)/shard_map/all_gather | solution.py:185
  8.7 687.4 %all-gather.9.cloned.1.call-start = ((), (), s32[]{:S(2)}) async-start(), calls=%async_computation.12 | async-start | bytes 5947392 | tf_op jit(solution)/shard_map/all_gather | solution.py:186
  9.4 698.6 %all-gather.11.cloned.1.call-start = ((), (), s32[]{:S(2)}) async-start(), calls=%async_computation.13 | async-start | bytes 5947392 | tf_op jit(solution)/shard_map/all_gather | solution.py:187
  10.0 1218.3 %reduce-scatter.15.cloned.1.call-start = ((), (), s32[]{:S(2)}) async-start(), calls=%async_computation.16 | async-start | bytes 540672 | tf_op jit(solution)/shard_map/reduce_scatter | solution.py:319
  86.0 290.5 %copy-start.4 = (bf16[1,1024,1024]{1,2,0:T(8,128)(2,1)}, bf16[1,1024,1024]{1,2,0:T(8,128)(2,1)S(1)}, u32[]{:S(2)}) copy-start(bf16[1,1024,1024]{1,2,0:T(8,128)(2,1)S(1)} %copy.193) | copy-start | bytes 6291460
  124.0 411.7 %copy-start.48 = (f32[1024]{0:T(1024)}, f32[1024]{0:T(1024)S(1)}, u32[]{:S(2)}) copy-start(f32[1024]{0:T(1024)S(1)} %convert_element_type.168) | copy-start | bytes 12292
  125.1 410.6 %copy-start.46 = (f32[1024]{0:T(1024)}, f32[1024]{0:T(1024)S(1)}, u32[]{:S(2)}) copy-start(f32[1024]{0:T(1024)S(1)} %get-tuple-element.381) | copy-start | bytes 12292
  205.9 172.3 %copy-start.21 = (f32[1024,32]{0,1:T(8,128)}, f32[1024,32]{0,1:T(8,128)S(1)}, u32[]{:S(2)}) copy-start(f32[1024,32]{0,1:T(8,128)S(1)} %get-tuple-element.384) | copy-start | bytes 393220
  205.9 172.3 %copy-start.23 = (f32[1024,32]{0,1:T(8,128)}, f32[1024,32]{0,1:T(8,128)S(1)}, u32[]{:S(2)}) copy-start(f32[1024,32]{0,1:T(8,128)S(1)} %get-tuple-element.385) | copy-start | bytes 393220
  233.1 69.6 %copy-start.53 = (bf16[32,128]{1,0:T(8,128)(2,1)S(1)}, bf16[32,128]{1,0:T(8,128)(2,1)}, u32[]{:S(2)}) copy-start(bf16[32,128]{1,0:T(8,128)(2,1)} %param.25) | copy-start | bytes 24580
  302.7 76.2 %copy-start.10 = (f32[1024,2,16]{2,1,0:T(2,128)}, f32[1024,2,16]{2,1,0:T(2,128)S(1)}, u32[]{:S(2)}) copy-start(f32[1024,2,16]{2,1,0:T(2,128)S(1)} %copy.204) | copy-start | bytes 393220
  399.2 68.3 %copy-start.55 = (bf16[32,128]{1,0:T(8,128)(2,1)S(1)}, bf16[32,128]{1,0:T(8,128)(2,1)}, u32[]{:S(2)}) copy-start(bf16[32,128]{1,0:T(8,128)(2,1)} %param.27) | copy-start | bytes 24580
  467.5 89.3 %copy-start.14 = (f32[1024,2,16]{2,1,0:T(2,128)}, f32[1024,2,16]{2,1,0:T(2,128)S(1)}, u32[]{:S(2)}) copy-start(f32[1024,2,16]{2,1,0:T(2,128)S(1)} %copy.210) | copy-start | bytes 393220
  534.8 22.0 copy-start.32
  582.5 15.3 copy-start
  582.5 15.3 copy-start.35
  633.7 15.3 copy-start
  633.7 15.3 copy-start.35
  729.9 11.4 copy-start.9
  729.9 11.4 copy-start.58
  729.9 11.4 copy-start.62
  741.3 9.3 copy-start.20
  758.5 18.4 copy-start.1
  758.5 18.4 copy-start.17
  872.2 18.3 copy-start.1
  872.2 18.3 copy-start.17
  985.8 8.2 copy-start.15
  994.0 9.7 copy-start.2
  994.0 9.8 copy-start.16
  1017.1 8.2 copy-start.11
  1025.4 10.6 copy-start.3
  1025.4 10.6 copy-start.13
  1050.2 26.1 copy-start.44
  1058.4 17.9 copy-start.5
  1058.4 17.9 copy-start.47
  1058.4 17.9 copy-start.49
  1077.9 263.5 %reduce-scatter.19.cloned.1.call-start = ((), (), s32[]{:S(2)}) async-start(), calls=%async_computation.18 | async-start | bytes 540672 | tf_op jit(solution)/shard_map/reduce_scatter | solution.py:319
  1084.9 389.6 %reduce-scatter.11.cloned.1.call-start = ((), (), s32[]{:S(2)}) async-start(), calls=%async_computation.14 | async-start | bytes 540672 | tf_op jit(solution)/shard_map/reduce_scatter | solution.py:319
  1086.6 521.0 %reduce-scatter.17.cloned.1.call-start = ((), (), s32[]{:S(2)}) async-start(), calls=%async_computation.17 | async-start | bytes 540672 | tf_op jit(solution)/shard_map/reduce_scatter | solution.py:319
  1089.2 651.4 %reduce-scatter.21.cloned.1.call-start = ((), (), s32[]{:S(2)}) async-start(), calls=%async_computation.19 | async-start | bytes 540672 | tf_op jit(solution)/shard_map/reduce_scatter | solution.py:319
  1107.3 733.3 %reduce-scatter.13.cloned.1.call-start = ((), (), s32[]{:S(2)}) async-start(), calls=%async_computation.15 | async-start | bytes 1622016 | tf_op jit(solution)/shard_map/reduce_scatter | solution.py:319
  1111.7 874.6 %reduce-scatter.23.cloned.1.call-start = ((), (), s32[]{:S(2)}) async-start(), calls=%async_computation.20 | async-start | bytes 4325376 | tf_op jit(solution)/shard_map/reduce_scatter | solution.py:319
  1119.0 1116.8 %reduce-scatter.25.cloned.1.call-start = ((), (), s32[]{:S(2)}) async-start(), calls=%async_computation.21 | async-start | bytes 11894784 | tf_op jit(solution)/shard_map/reduce_scatter | solution.py:242
  1130.8 1356.4 %reduce-scatter.27.cloned.1.call-start = ((), (), s32[]{:S(2)}) async-start(), calls=%async_computation.22 | async-start | bytes 11894784 | tf_op jit(solution)/shard_map/reduce_scatter | solution.py:242
  1142.7 1595.7 %reduce-scatter.29.cloned.1.call-start = ((), (), s32[]{:S(2)}) async-start(), calls=%async_computation.23 | async-start | bytes 11894784 | tf_op jit(solution)/shard_map/reduce_scatter | solution.py:248
  (34 other events, 98.2 us)
Sparse Core Ops, SparseCore 0:
  11.0 59.9 all-gather.4
  73.9 67.7 all-gather.6
  144.6 68.0 all-gather.8
  215.5 68.7 all-gather.10
  1078.0 130.2 reduce-scatter.14
  1211.1 130.3 reduce-scatter.18
  1344.3 130.2 reduce-scatter.10
  1477.4 130.1 reduce-scatter.16
  1610.5 130.1 reduce-scatter.20
  1747.2 93.3 reduce-scatter.12
  1843.5 142.6 reduce-scatter.22
  1989.1 246.6 reduce-scatter.24
  2238.8 248.3 reduce-scatter.26
  2490.1 248.3 reduce-scatter.28
where the time goes:
time: 2760 us; the launch traced here: 2750 us
  waiting for transfers between devices  1510 us (55%)
  matrix products  516 us (19%)
  blocking collectives  491 us (18%)
  other arithmetic  101 us (4%)
  local copies, waits for them, and re-layouts  99.8 us (4%)
    reduce_scatter x7, waiting for transfers between devices, on_device(): lax.psum_scatter((grad_norm_gain, outer_sum(normed_cols, grad_flats[0]),...  758 us
    reduce_scatter x2, waiting for transfers between devices, on_device(): lax.psum_scatter((grad_mlp_gain, outer_sum(normed_cols, grad_gate), outer...  501 us
    reduce_scatter x1, waiting for transfers between devices, on_device(): lax.psum_scatter(outer_sum(inner_act, cotangent), ('dp', 'fsdp'), scatter...  251 us
    unnamed x2, blocking collectives  74.6 us
    all_gather x1, blocking collectives, on_device(): lax.all_gather(w_query_dims, ('dp', 'fsdp'), axis=0, tiled=True)  73.5 us
    all_gather x1, blocking collectives, on_device(): lax.all_gather(w_query_heads, ('dp', 'fsdp'), axis=0, tiled=True)  72.2 us
    all_gather x1, blocking collectives, on_device(): lax.all_gather(w_key_dims, ('dp', 'fsdp'), axis=0, tiled=True)  72 us
    all_gather x1, blocking collectives, on_device(): lax.all_gather(w_value_dims, ('dp', 'fsdp'), axis=0, tiled=True)  67.3 us
  transfers between devices with their start and end apart: 14, of which 9 were waited for; matrix products, arithmetic and copies ran while one was open for 12% of the time, Pallas kernels for 0%

commit v1 on v0

--- a/solution.py
+++ b/solution.py
@@ -1,15 +1,21 @@
+import functools
 import math
 
 import jax
 import jax.numpy as jnp
 from jax import lax
+from jax.experimental import pallas as pl
+from jax.experimental.pallas import tpu as pltpu
 from jax.sharding import PartitionSpec as P
+
+MESH = pl.DeviceIdType.MESH
 
 D = 1024
 H = 16
 DH = 64
 RQ = 6
 RK = 2
+PACKED = 896
 
 
 epsilon = 1e-06
@@ -84,9 +90,431 @@
     grad_heads = jnp.einsum("bshd,bsrd->bsrh", grad_full, dims_act, precision=highest) / rank_count
     grad_dims = jnp.einsum("bshd,bsrh->bsrd", grad_full, heads_act, precision=highest) / rank_count
     return (grad_heads, grad_dims)
+ANY = pl.BlockSpec(memory_space=pl.ANY)
+
+
+def grid_of(mesh):
+    nd, nf = mesh.shape["dp"], mesh.shape["fsdp"]
+    nc = math.gcd(2, nd)
+    nz = math.gcd(4, nf)
+    return (nd // nc, nc, nz, nf // nz)
+
+
+class Place:
+    def __init__(self, dims):
+        self.dims = dims
+        ny, nc, nz, nx = dims
+        dp, fs = lax.axis_index("dp"), lax.axis_index("fsdp")
+        self.y, self.c = lax.div(dp, nc), lax.rem(dp, nc)
+        self.z, self.x = lax.div(fs, nx), lax.rem(fs, nx)
+
+    def at(self, axis, k):
+        n = self.dims["yczx".index(axis)]
+        return lax.rem(getattr(self, axis) + k + n, n)
+
+    def device(self, axis=None, k=0):
+        ny, nc, nz, nx = self.dims
+        put = {a: getattr(self, a) for a in "yczx"}
+        if axis is not None:
+            put[axis] = self.at(axis, k)
+        return (put["y"] * nc + put["c"], put["z"] * nx + put["x"])
+
+
+def peers_of(dims):
+    ny, nc, nz, nx = dims
+    return [(a, k) for a, n in (("y", ny), ("c", nc), ("z", nz), ("x", nx)) for k in range(1, n)]
+
+
+def enter(place):
+    barrier = pltpu.get_barrier_semaphore()
+    peers = peers_of(place.dims)
+    for axis, k in peers:
+        pl.semaphore_signal(barrier, inc=1, device_id=place.device(axis, k), device_id_type=MESH)
+    pl.semaphore_wait(barrier, len(peers))
+
+
+class Gather:
+    def __init__(self, place, src, dst, sems, i):
+        self.p, self.src, self.dst, self.i = place, src, dst, i
+        self.local, self.zs, self.zr, self.as_, self.ar, self.bs, self.br, self.cs, self.cr = sems
+
+    @staticmethod
+    def sem_shapes(dims, n):
+        ny, nc, nz, nx = dims
+        dma = pltpu.SemaphoreType.DMA
+        m = max(nx, ny) - 1
+        one = lambda k: dma((n, max(1, k)))
+        return [dma((n,)), one(nz - 1), one(nz - 1), one(m), one(m), one(m), one(m), one(nx + ny - 1), one(nx + ny - 1)]
+
+    def copy(self, ref_src, ref_dst, send, recv, axis, k):
+        return pltpu.make_async_remote_copy(
+            src_ref=ref_src, dst_ref=ref_dst, send_sem=send, recv_sem=recv,
+            device_id=self.p.device(axis, k), device_id_type=MESH,
+        )
+
+    def z_copies(self):
+        p, i = self.p, self.i
+        nz = p.dims[2]
+        mine = self.dst.at[p.y, p.c, p.z, p.x]
+        def one(k, back):
+            if back:
+                ref = self.dst.at[p.y, p.c, p.at("z", -k), p.x]
+                return self.copy(ref, ref, self.zs.at[i, k - 1], self.zr.at[i, k - 1], "z", k)
+            return self.copy(self.src, mine, self.zs.at[i, k - 1], self.zr.at[i, k - 1], "z", k)
+
+        return [[functools.partial(one, k, back) for k in range(1, nz)] for back in (False, True)]
+
+    def part(self, first, step, y, x, c):
+        every = slice(None)
+        if step == 0:
+            return self.dst.at[y, c, :, x]
+        return self.dst.at[y, c] if first == "x" else self.dst.at[:, c, :, x]
+
+    def side_copies(self, first, step):
+        p, i = self.p, self.i
+        axis = first if step == 0 else {"x": "y", "y": "x"}[first]
+        n = p.dims["yczx".index(axis)]
+        s, r = ((self.as_, self.ar), (self.bs, self.br))[step]
+
+        def one(k, back):
+            y, x = p.y, p.x
+            if back:
+                y, x = (p.y, p.at("x", -k)) if axis == "x" else (p.at("y", -k), p.x)
+            ref = self.part(first, step, y, x, p.c)
+            return self.copy(ref, ref, s.at[i, k - 1], r.at[i, k - 1], axis, k)
+
+        return [[functools.partial(one, k, back) for k in range(1, n)] for back in (False, True)]
+
+    def core_copies(self, first, c):
+        p, i = self.p, self.i
+        second = {"x": "y", "y": "x"}[first]
+        lists, j = [], 0
+        for step, axis in ((0, None), (0, first), (1, second)):
+            now = []
+            count = 1 if axis is None else p.dims["yczx".index(axis)] - 1
+            for k in range(1, count + 1):
+                def one(axis=axis, step=step, k=k, j=j):
+                    y = p.at("y", -k) if axis == "y" else p.y
+                    x = p.at("x", -k) if axis == "x" else p.x
+                    ref = self.part(first, step, y, x, c)
+                    return self.copy(ref, ref, self.cs.at[i, j], self.cr.at[i, j], "c", 1)
+
+                now.append(one)
+                j += 1
+            lists.append(now)
+        return lists
+
+    def start(self):
+        p = self.p
+        mine = self.dst.at[p.y, p.c, p.z, p.x]
+        pltpu.make_async_copy(self.src, mine, self.local.at[self.i]).start()
+        for copy in self.z_copies()[0]:
+            copy().start()
+
+    def by_core(self, body):
+        if self.p.dims[1] == 1:
+            body("x")
+            return
+        pl.when(self.p.c == 0)(lambda: body("x"))
+        pl.when(self.p.c == 1)(lambda: body("y"))
+
+    def after_z(self):
+        p = self.p
+        mine = self.dst.at[p.y, p.c, p.z, p.x]
+        pltpu.make_async_copy(self.src, mine, self.local.at[self.i]).wait()
+        for copy in self.z_copies()[1]:
+            copy().wait_recv()
+
+        def body(first):
+            for copy in self.side_copies(first, 0)[0]:
+                copy().start()
+            if p.dims[1] > 1:
+                for copy in self.core_copies(first, p.c)[0]:
+                    copy().start()
+
+        self.by_core(body)
+
+    def after_first(self):
+        p = self.p
+
+        def body(first):
+            for copy in self.side_copies(first, 0)[1]:
+                copy().wait_recv()
+            for copy in self.side_copies(first, 1)[0]:
+                copy().start()
+            if p.dims[1] > 1:
+                for copy in self.core_copies(first, p.c)[1]:
+                    copy().start()
+
+        self.by_core(body)
+
+    def after_second(self):
+        p = self.p
+
+        def body(first):
+            for copy in self.side_copies(first, 1)[1]:
+                copy().wait_recv()
+            if p.dims[1] > 1:
+                for copy in self.core_copies(first, p.c)[2]:
+                    copy().start()
+
+        self.by_core(body)
+
+    def finish(self):
+        p = self.p
+        for copy in self.z_copies()[0]:
+            copy().wait_send()
+
+        def body(first):
+            for step in (0, 1):
+                for copy in self.side_copies(first, step)[0]:
+                    copy().wait_send()
+            if p.dims[1] > 1:
+                for now in self.core_copies(first, p.c):
+                    for copy in now:
+                        copy().wait_send()
+                other = {"x": "y", "y": "x"}[first]
+                for now in self.core_copies(other, p.at("c", 1)):
+                    for copy in now:
+                        copy().wait_recv()
+
+        self.by_core(body)
+
+    def stages(self):
+        return [self.start, self.after_z, self.after_first, self.after_second, self.finish]
+
+
+def gather_kernel(dims, n, *refs):
+    place = Place(dims)
+    src, dst, sems = refs[:n], refs[n:2 * n], refs[2 * n:]
+    enter(place)
+    jobs = [Gather(place, src[i], dst[i], sems, i).stages() for i in range(n)]
+    run_stages(jobs)
+
+
+def gather(dims, arrays, collective_id):
+    n = len(arrays)
+    outs = pl.pallas_call(
+        functools.partial(gather_kernel, dims, n),
+        out_shape=[jax.ShapeDtypeStruct(dims + a.shape, a.dtype) for a in arrays],
+        in_specs=[ANY] * n,
+        out_specs=[ANY] * n,
+        scratch_shapes=Gather.sem_shapes(dims, n),
+        compiler_params=pltpu.CompilerParams(collective_id=collective_id, has_side_effects=True),
+        name="gather_weights",
+    )(*arrays)
+    return [o.reshape((-1,) + a.shape[1:]) for o, a in zip(outs, arrays)]
+
+
+class Scatter:
+    def __init__(self, place, src, out, bufs, sems, i):
+        self.p, self.src, self.out, self.i = place, src, out, i
+        self.own, self.from_core, self.from_a, self.from_b, self.from_z = bufs
+        self.local, self.cs, self.cr, self.as_, self.ar, self.bs, self.br, self.zs, self.zr = sems
+
+    @staticmethod
+    def sem_shapes(dims, n):
+        ny, nc, nz, nx = dims
+        dma = pltpu.SemaphoreType.DMA
+        m = max(nx, ny, 2) - 1
+        return [dma((n, nx))] * 3 + [dma((n, m))] * 4 + [dma((n, max(1, nz - 1)))] * 2
+
+    @staticmethod
+    def buf_shapes(dims, block):
+        ny, nc, nz, nx = dims
+        m = max(nx, ny, 2)
+        buf = lambda *s: pltpu.VMEM(s + block, jnp.bfloat16)
+        return [buf(ny, nx, nz), buf(ny, nx, nz), buf(m - 1, m, nz), buf(m - 1, nz), buf(max(1, nz - 1))]
+
+    def copy(self, src, dst, send, recv, axis, k):
+        return pltpu.make_async_remote_copy(
+            src_ref=src, dst_ref=dst, send_sem=send, recv_sem=recv,
+            device_id=self.p.device(axis, k), device_id_type=MESH,
+        )
+
+    def loads(self):
+        p, i = self.p, self.i
+        for x in range(p.dims[3]):
+            yield lambda x=x: pltpu.make_async_copy(self.src.at[:, p.c, :, x], self.own.at[:, x], self.local.at[i, x])
+
+    def core_copies(self):
+        p, i = self.p, self.i
+        if p.dims[1] == 1:
+            return
+        for x in range(p.dims[3]):
+            yield lambda x=x: self.copy(
+                self.src.at[:, p.at("c", 1), :, x], self.from_core.at[:, x], self.cs.at[i, x], self.cr.at[i, x], "c", 1)
+
+    def a_copies(self, first):
+        p, i = self.p, self.i
+        ny, nc, nz, nx = p.dims
+        for k in range(1, ny if first == "y" else nx):
+            def copy(k=k):
+                if first == "y":
+                    src, dst = self.own.at[p.at("y", k)], self.from_a.at[k - 1, pl.ds(0, nx)]
+                else:
+                    src, dst = self.own.at[:, p.at("x", k)], self.from_a.at[k - 1, pl.ds(0, ny)]
+                return self.copy(src, dst, self.as_.at[i, k - 1], self.ar.at[i, k - 1], first, k)
+            yield copy
+
+    def b_copies(self, first):
+        p, i = self.p, self.i
+        ny, nc, nz, nx = p.dims
+        second = {"x": "y", "y": "x"}[first]
+        for k in range(1, ny if second == "y" else nx):
+            def copy(k=k):
+                src = self.own.at[p.at("y", k), p.x] if second == "y" else self.own.at[p.y, p.at("x", k)]
+                return self.copy(src, self.from_b.at[k - 1], self.bs.at[i, k - 1], self.br.at[i, k - 1], second, k)
+            yield copy
+
+    def z_copies(self):
+        p, i = self.p, self.i
+        for k in range(1, p.dims[2]):
+            yield lambda k=k: self.copy(
+                self.own.at[p.y, p.x, p.at("z", k)], self.from_z.at[k - 1], self.zs.at[i, k - 1], self.zr.at[i, k - 1], "z", k)
+
+    def by_core(self, body):
+        if self.p.dims[1] == 1:
+            body("y")
+            return
+        pl.when(self.p.c == 0)(lambda: body("y"))
+        pl.when(self.p.c == 1)(lambda: body("x"))
+
+    @staticmethod
+    def add(total, terms):
+        value = total[...].astype(jnp.float32)
+        for term in terms:
+            value = value + term[...].astype(jnp.float32)
+        return value
+
+    def start(self):
+        for copy in self.core_copies():
+            copy().start()
+        for copy in self.loads():
+            copy().start()
+
+    def after_core(self):
+        p = self.p
+        ny, nc, nz, nx = p.dims
+        for copy in self.loads():
+            copy().wait()
+        for copy in self.core_copies():
+            copy().wait_recv()
+        if nc > 1:
+            def body(t, carry):
+                at = (lax.div(t, nx * nz), lax.rem(lax.div(t, nz), nx), lax.rem(t, nz))
+                self.own[at] = self.add(self.own.at[at], [self.from_core.at[at]]).astype(jnp.bfloat16)
+                return carry
+            lax.fori_loop(0, ny * nx * nz, body, 0)
+
+        def go(first):
+            for copy in self.a_copies(first):
+                copy().start()
+        self.by_core(go)
+
+    def after_a(self):
+        p = self.p
+        ny, nc, nz, nx = p.dims
+
+        def go(first):
+            for copy in self.a_copies(first):
+                copy().wait_recv()
+            n = ny if first == "y" else nx
+
+            def body(t, carry):
+                j, z = lax.div(t, nz), lax.rem(t, nz)
+                at = (p.y, j, z) if first == "y" else (j, p.x, z)
+                terms = [self.from_a.at[k, j, z] for k in range(n - 1)]
+                self.own[at] = self.add(self.own.at[at], terms).astype(jnp.bfloat16)
+                return carry
+            if n > 1:
+                lax.fori_loop(0, (nx if first == "y" else ny) * nz, body, 0)
+            for copy in self.b_copies(first):
+                copy().start()
+        self.by_core(go)
+
+    def after_b(self):
+        p = self.p
+        ny, nc, nz, nx = p.dims
+
+        def go(first):
+            for copy in self.b_copies(first):
+                copy().wait_recv()
+            n = nx if first == "y" else ny
+
+            def body(z, carry):
+                at = (p.y, p.x, z)
+                terms = [self.from_b.at[k, z] for k in range(n - 1)]
+                self.own[at] = self.add(self.own.at[at], terms).astype(jnp.bfloat16)
+                return carry
+            if n > 1:
+                lax.fori_loop(0, nz, body, 0)
+        self.by_core(go)
+        for copy in self.z_copies():
+            copy().start()
+
+    def after_z(self):
+        p = self.p
+        for copy in self.z_copies():
+            copy().wait_recv()
+        terms = [self.from_z.at[k] for k in range(p.dims[2] - 1)]
+        self.out[...] = self.add(self.own.at[p.y, p.x, p.z], terms)
+
+    def finish(self):
+        for copy in self.core_copies():
+            copy().wait_send()
+
+        def go(first):
+            for copy in self.a_copies(first):
+                copy().wait_send()
+            for copy in self.b_copies(first):
+                copy().wait_send()
+        self.by_core(go)
+        for copy in self.z_copies():
+            copy().wait_send()
+
+    def stages(self):
+        return [self.start, self.after_core, self.after_a, self.after_b, self.after_z, self.finish]
+
+
+def run_stages(jobs):
+    n, depth = len(jobs), len(jobs[0])
+    for t in range(n + depth - 1):
+        for i in range(n):
+            if 0 <= t - i < depth:
+                jobs[i][t - i]()
+
+
+def scatter_kernel(dims, n, *refs):
+    place = Place(dims)
+    src, out, rest = refs[:n], refs[n:2 * n], refs[2 * n:]
+    bufs, sems = rest[:5 * n], rest[5 * n:]
+    enter(place)
+    run_stages([Scatter(place, src[i], out[i], bufs[5 * i:5 * i + 5], sems, i).stages() for i in range(n)])
+
+
+def scatter(dims, arrays, collective_id):
+    n = len(arrays)
+    devices = math.prod(dims)
+    blocks = [(a.shape[0] // devices,) + a.shape[1:] for a in arrays]
+    shaped = [a.reshape(dims + b) for a, b in zip(arrays, blocks)]
+    scratch = []
+    for b in blocks:
+        scratch += Scatter.buf_shapes(dims, b)
+    return pl.pallas_call(
+        functools.partial(scatter_kernel, dims, n),
+        out_shape=[jax.ShapeDtypeStruct(b, jnp.float32) for b in blocks],
+        in_specs=[ANY] * n,
+        out_specs=[pl.BlockSpec(memory_space=pltpu.VMEM)] * n,
+        scratch_shapes=scratch + Scatter.sem_shapes(dims, n),
+        compiler_params=pltpu.CompilerParams(
+            collective_id=collective_id, has_side_effects=True, vmem_limit_bytes=56 << 20),
+        name="scatter_gradients",
+    )(*shaped)
 
 
 def on_device(
+    dims,
     tokens,
     doc_ids,
     norm_gain,
@@ -112,26 +540,23 @@
     block_count = seq_len // block_len
     positions = jnp.arange(seq_len, dtype=jnp.int32)
     starts = jnp.arange(block_count) * block_len
-    attn_full = (
-        lax.all_gather(norm_gain, ("dp", "fsdp"), axis=0, tiled=True),
-        lax.all_gather(w_query_heads, ("dp", "fsdp"), axis=0, tiled=True),
-        lax.all_gather(w_query_dims, ("dp", "fsdp"), axis=0, tiled=True),
-        lax.all_gather(w_key_heads, ("dp", "fsdp"), axis=0, tiled=True),
-        lax.all_gather(w_key_dims, ("dp", "fsdp"), axis=0, tiled=True),
-        lax.all_gather(w_value_heads, ("dp", "fsdp"), axis=0, tiled=True),
-        lax.all_gather(w_value_dims, ("dp", "fsdp"), axis=0, tiled=True),
-        lax.all_gather(w_output, ("dp", "fsdp"), axis=0, tiled=True),
-    )
-    (
-        gain_one,
-        query_heads_w,
-        query_dims_w,
-        key_heads_w,
-        key_dims_w,
-        value_heads_w,
-        value_dims_w,
-        output_w,
-    ) = attn_full
+    parts = (w_query_heads, w_query_dims, w_key_heads, w_key_dims, w_value_heads, w_value_dims)
+    edges = [0]
+    for part in parts:
+        edges.append(edges[-1] + part.shape[1])
+    packed = jnp.concatenate(
+        parts
+        + (norm_gain[:, None], mlp_gain[:, None])
+        + (jnp.zeros((norm_gain.shape[0], PACKED - edges[-1] - 2), jnp.bfloat16),),
+        axis=1,
+    )
+    packed_w, output_w, gate_w, up_w, down_w = gather(
+        dims, [packed, w_output, w_gate, w_up, w_down], 0
+    )
+    query_heads_w, query_dims_w, key_heads_w, key_dims_w, value_heads_w, value_dims_w = [
+        packed_w[:, lo:hi] for lo, hi in zip(edges, edges[1:])
+    ]
+    gain_one, gain_two = packed_w[:, edges[-1]], packed_w[:, edges[-1] + 1]
     inputs_flat = tokens.astype(jnp.float32).reshape(token_count, D)
     scale_one = rms_scale(inputs_flat)
     normed = (inputs_flat * scale_one * gain_one.astype(jnp.float32)).astype(jnp.bfloat16)
@@ -180,13 +605,6 @@
     mixed_blocks, lse_blocks = lax.map(forward_block, starts)
     mixed_heads = jnp.moveaxis(mixed_blocks, 0, 1).reshape(token_count, H * DH)
     middle = inputs_flat + forward_dot(mixed_heads, output_w)
-    mlp_full = (
-        lax.all_gather(mlp_gain, ("dp", "fsdp"), axis=0, tiled=True),
-        lax.all_gather(w_gate, ("dp", "fsdp"), axis=0, tiled=True),
-        lax.all_gather(w_up, ("dp", "fsdp"), axis=0, tiled=True),
-        lax.all_gather(w_down, ("dp", "fsdp"), axis=0, tiled=True),
-    )
-    gain_two, gate_w, up_w, down_w = mlp_full
     scale_two = rms_scale(middle)
     gain_two_f = gain_two.astype(jnp.float32)
     normed_two = (middle * scale_two * gain_two_f).astype(jnp.bfloat16)
@@ -197,41 +615,14 @@
     inner_act = (silu_gate * up_proj).astype(jnp.bfloat16)
     result = middle + forward_dot(inner_act, down_w)
     output = result.astype(jnp.bfloat16).reshape(tokens.shape)
-    mlp_back = (
-        lax.all_gather(mlp_gain, ("dp", "fsdp"), axis=0, tiled=True),
-        lax.all_gather(w_gate, ("dp", "fsdp"), axis=0, tiled=True),
-        lax.all_gather(w_up, ("dp", "fsdp"), axis=0, tiled=True),
-        lax.all_gather(w_down, ("dp", "fsdp"), axis=0, tiled=True),
-    )
-    attn_back = (
-        lax.all_gather(norm_gain, ("dp", "fsdp"), axis=0, tiled=True),
-        lax.all_gather(w_query_heads, ("dp", "fsdp"), axis=0, tiled=True),
-        lax.all_gather(w_query_dims, ("dp", "fsdp"), axis=0, tiled=True),
-        lax.all_gather(w_key_heads, ("dp", "fsdp"), axis=0, tiled=True),
-        lax.all_gather(w_key_dims, ("dp", "fsdp"), axis=0, tiled=True),
-        lax.all_gather(w_value_heads, ("dp", "fsdp"), axis=0, tiled=True),
-        lax.all_gather(w_value_dims, ("dp", "fsdp"), axis=0, tiled=True),
-        lax.all_gather(w_output, ("dp", "fsdp"), axis=0, tiled=True),
-    )
-    gain_two_b, gate_wb, up_wb, down_wb = mlp_back
-    (
-        gain_one_b,
-        query_heads_wb,
-        query_dims_wb,
-        key_heads_wb,
-        key_dims_wb,
-        value_heads_wb,
-        value_dims_wb,
-        output_wb,
-    ) = attn_back
     cotangent = out_grad.reshape(token_count, D)
-    grad_inner = back_dot(cotangent, down_wb)
+    grad_inner = back_dot(cotangent, down_w)
     grad_gate = (
         grad_inner * up_proj * sigmoid_gate * (1.0 + gate_proj * (1.0 - sigmoid_gate))
     ).astype(jnp.bfloat16)
     grad_up = (grad_inner * silu_gate).astype(jnp.bfloat16)
-    grad_normed_two = back_dot(grad_gate, gate_wb) + back_dot(grad_up, up_wb)
-    gained_two = grad_normed_two * gain_two_b.astype(jnp.float32)
+    grad_normed_two = back_dot(grad_gate, gate_w) + back_dot(grad_up, up_w)
+    gained_two = grad_normed_two * gain_two.astype(jnp.float32)
     grad_mlp_gain = jnp.sum(grad_normed_two * middle * scale_two, axis=0)
     grad_middle = (
         cotangent.astype(jnp.float32)
@@ -239,18 +630,9 @@
         - middle * scale_two**3 * jnp.mean(gained_two * middle, axis=-1, keepdims=True)
     )
     normed_cols = normed_two
-    mlp_grads = lax.psum_scatter(
-        (grad_mlp_gain, outer_sum(normed_cols, grad_gate), outer_sum(normed_cols, grad_up)),
-        ("dp", "fsdp"),
-        scatter_dimension=0,
-        tiled=True,
-    )
-    down_grad = lax.psum_scatter(
-        outer_sum(inner_act, cotangent), ("dp", "fsdp"), scatter_dimension=0, tiled=True
-    )
     grad_branch = grad_middle.astype(jnp.bfloat16)
     grad_mixed = (
-        back_dot(grad_branch, output_wb).astype(jnp.bfloat16).reshape(row_count, seq_len, H, DH)
+        back_dot(grad_branch, output_w).astype(jnp.bfloat16).reshape(row_count, seq_len, H, DH)
     )
 
     def backward_block(carry_grads, block_inputs):
@@ -294,12 +676,12 @@
     grad_dims_query = rotate_back(grad_dims_query, cosine_table, sine_table)
     grad_dims_key = rotate_back(grad_dims_key, cosine_table, sine_table)
     factor_pairs = (
-        (grad_heads_query, query_heads_wb),
-        (grad_dims_query, query_dims_wb),
-        (grad_heads_key, key_heads_wb),
-        (grad_dims_key, key_dims_wb),
-        (grad_heads_value, value_heads_wb),
-        (grad_dims_value, value_dims_wb),
+        (grad_heads_query, query_heads_w),
+        (grad_dims_query, query_dims_w),
+        (grad_heads_key, key_heads_w),
+        (grad_dims_key, key_dims_w),
+        (grad_heads_value, value_heads_w),
+        (grad_dims_value, value_dims_w),
     )
     grad_flats = []
     grad_normed = jnp.zeros((token_count, D), jnp.float32)
@@ -307,7 +689,7 @@
         grad_flat = grad_factor.reshape(token_count, weight.shape[1]).astype(jnp.bfloat16)
         grad_flats.append(grad_flat)
         grad_normed = grad_normed + back_dot(grad_flat, weight)
-    gained_one = grad_normed * gain_one_b.astype(jnp.float32)
+    gained_one = grad_normed * gain_one.astype(jnp.float32)
     grad_norm_gain = jnp.sum(grad_normed * inputs_flat * scale_one, axis=0)
     grad_inputs = (
         grad_middle
@@ -316,42 +698,41 @@
     )
     grad_tokens = grad_inputs.astype(jnp.bfloat16).reshape(tokens.shape)
     normed_cols = normed
-    attn_grads = lax.psum_scatter(
-        (
-            grad_norm_gain,
-            outer_sum(normed_cols, grad_flats[0]),
-            outer_sum(normed_cols, grad_flats[1]),
-            outer_sum(normed_cols, grad_flats[2]),
-            outer_sum(normed_cols, grad_flats[3]),
-            outer_sum(normed_cols, grad_flats[4]),
-            outer_sum(normed_cols, grad_flats[5]),
-            outer_sum(mixed_heads, grad_branch),
-        ),
-        ("dp", "fsdp"),
-        scatter_dimension=0,
-        tiled=True,
-    )
+    packed_grad = jnp.concatenate(
+        [outer_sum(normed_cols, jnp.concatenate(grad_flats, axis=1))]
+        + [grad_norm_gain[:, None], grad_mlp_gain[:, None]]
+        + [jnp.zeros((D, PACKED - edges[-1] - 2), jnp.float32)],
+        axis=1,
+    )
+    low = lambda v: v.astype(jnp.bfloat16)
+    gate_out, up_out, down_out, output_out, packed_out = scatter(
+        dims,
+        [
+            low(outer_sum(normed_two, grad_gate)),
+            low(outer_sum(normed_two, grad_up)),
+            low(outer_sum(inner_act, cotangent)),
+            low(outer_sum(mixed_heads, grad_branch)),
+            low(packed_grad),
+        ],
+        1,
+    )
+    parts_out = [packed_out[:, lo:hi] for lo, hi in zip(edges, edges[1:])]
     return (
         output,
         grad_tokens,
-        attn_grads[0],
-        attn_grads[1],
-        attn_grads[2],
-        attn_grads[3],
-        attn_grads[4],
-        attn_grads[5],
-        attn_grads[6],
-        attn_grads[7],
-        mlp_grads[0],
-        mlp_grads[1],
-        mlp_grads[2],
-        down_grad,
+        packed_out[:, edges[-1]],
+        *parts_out,
+        output_out,
+        packed_out[:, edges[-1] + 1],
+        gate_out,
+        up_out,
+        down_out,
     )
 
 
 def solution(mesh):
     return jax.shard_map(
-        on_device,
+        functools.partial(on_device, grid_of(mesh)),
         mesh=mesh,
         in_specs=(
             P(("dp", "fsdp"), None, None),

time: 2760 us -> 979 us (0.35)
  waiting for transfers between devices: 1510 us -> 0 us
  blocking collectives: 491 us -> 0 us
  Pallas kernels: 0 us -> 248 us
  matrix products: 516 us -> 484 us
    reduce_scatter x10 -> x0, waiting for transfers between devices: 1510 us -> none  [the longest x7 758 us: on_device(): lax.psum_scatter((grad_norm_gain, outer_sum(normed_cols, grad_flats[0]),...]
    all_gather x6 -> x0, blocking collectives: 416 us -> none  [the longest x1 73.5 us: on_device(): lax.all_gather(w_query_dims, ('dp', 'fsdp'), axis=0, tiled=True)]
    pallas_call x0 -> x2, Pallas kernels: none -> 248 us  [the longest x1 135 us: scatter(): pl.pallas_call(functools.partial(scatter_kernel, dims, n), out_shape=[jax...]
    unnamed x2 -> x0, blocking collectives: 74.6 us -> none
  transfers between devices with their start and end apart: 14 -> 0, of which waited for: 9 -> 0; matrix products, arithmetic and copies ran while one was open for 12% -> 0% of each run, Pallas kernels for 0% -> 0%
where the time goes in v1:
time: 979 us; the launch traced here: 969 us
  matrix products  484 us (49%)
  Pallas kernels  248 us (25%)
  local copies, waits for them, and re-layouts  116 us (12%)
  other arithmetic  110 us (11%)
    pallas_call x1, Pallas kernels, scatter(): pl.pallas_call(functools.partial(scatter_kernel, dims, n), out_shape=[jax...  135 us
    pallas_call x1, Pallas kernels, gather(): pl.pallas_call(functools.partial(gather_kernel, dims, n), out_shape=[jax....  114 us
    dot_general x4, matrix products, block_scores(): jnp.einsum('bqhd,bkhd->bhqk', query_block, key_full, preferred_element_ty...  68.3 us
    dot_general x10, matrix products, back_dot(): lax.dot_general(grad_rows, weight, (((1,), (1,)), ((), ())), preferred_el...  63.7 us
    convert_element_type x2, other arithmetic, backward_block(): grad_scores = (probs * (grad_probs - row_delta)).astype(jnp.bfloat16)  55.6 us
    dot_general x2, matrix products, backward_block(): jnp.einsum('bqhd,bkhd->bhqk', grad_mixed_block, value_full, preferred_ele...  52 us
    dot_general x3, matrix products, combine_factors(): jnp.einsum('bsrh,bsrd->bshd', heads_act, dims_act, precision=highest)  46.7 us
    dot_general x3, matrix products, split_factors(): jnp.einsum('bshd,bsrd->bsrh', grad_full, dims_act, precision=highest)  42.5 us

profile of v1, /device:TPU:0, one launch (start us, length us, event | category | flops | bytes accessed | tf_op | source)
XLA Modules:
  0.0 969.4 jit_solution(457703736737609056)
XLA Ops:
  13.1 113.7 %gather_weights.1 = (bf16[2,2,4,2,32,896]{5,4,3,2,1,0:T(8,128)(2,1)}, bf16[2,2,4,2,32,1024]{5,4,3,2,1,0:T(8,128)(2,1)}, bf16[2,2,4,2,32,2816]{5,4,3,2,1,0:T(8,12...) custom-call(bf16[32,896]{1,0:T(8,128)(2,1)} %concatenate.29.refs_0_, ...), custom_call_target="tpu_custom_call" | custom-call | tf_op jit(solution)/shard_map/gather_weights/pallas_call | solution.py:297
  156.0 16.7 %fusion.76 = bf16[1,1024,16,64]{3,2,1,0:T(8,128)(2,1)} fusion(f32[1024,6,16]{2,1,0:T(8,128)} %copy.157, f32[1024,6,64]{2,1,0:T(8,128)} %copy.158), kind=kOutput, calls=%fused_computation.92 | convolution fusion | flops 77594624 | bytes 4063232 | tf_op jit(solution)/shard_map/bsrh,bsrd->bshd/dot_general | solution.py:86
  172.7 5.5 copy.171
  178.1 14.8 %fusion.78 = bf16[1,1024,16,64]{3,2,1,0:T(8,128)(2,1)} fusion(f32[1024,2,16]{2,1,0:T(2,128)S(1)} %copy.169, f32[1024,2,64]{2,1,0:T(2,128)S(1)} %copy.170), kind=kOutput, calls=%fused_computation.94 | convolution fusion | flops 27262976 | bytes 2752512 | tf_op jit(solution)/shard_map/bsrh,bsrd->bshd/dot_general | solution.py:86
  192.9 5.6 copy.173
  198.5 15.2 %fusion.77 = bf16[1,1024,16,64]{3,2,1,0:T(8,128)(2,1)} fusion(f32[1024,2,16]{2,1,0:T(2,128)S(1)} %copy-done.19, f32[1024,2,64]{2,1,0:T(2,128)S(1)} %copy.164), kind=kOutput, calls=%fused_computation.93 | convolution fusion | flops 27262976 | bytes 2752512 | tf_op jit(solution)/shard_map/bsrh,bsrd->bshd/dot_general | solution.py:86
  213.8 5.6 copy.172
  219.4 100.9 %while.28 = (s32[]{:T(128)}, bf16[2,1,512,16,64]{2,4,3,1,0:T(8,128)(2,1)S(1)}, f32[2,1,16,512]{3,2,1,0:T(8,128)S(1)}, s32[2]{0:T(128)S(1)}, s32[1,1024]{1,0:T(1,...) while((s32[]{:T(128)}, ...), condition=%wide.region_4.5_spmd.clone, body=%wide.region_1.4_spmd.clone.sunk | while | flops 2250236416 | bytes 109328560 | solution.py:605
  223.3 16.5 %fusion.192 = (f32[16,512]{1,0:T(8,128)S(1)}, f32[16,512,1024]{2,1,0:T(8,128)}) fusion(pred[512,1024]{1,0:T(8,128)(4,1)S(1)} %fusion.191, bf16[1,1024,16,64]{1,3,2,0:T(8,128)(2,1)} %get-tuple-element.539, bf16[1,1024,16,64]{1,3,2,0:T(8,128)(2,1)} %get-tuple-element.538, s32[]{:T(128)S(6)} %select_n.59), kind=kOutput, calls=%fused_computation.5.clone.1 | convolution fusion | flops 1098899456 | bytes 37257220 | tf_op jit(solution)/shard_map/while/body/eval_jaxpr/bqhd,bkhd->bhqk/dot_general | solution.py:585
  239.9 14.9 %fusion.193 = f32[16,512]{1,0:T(8,128)S(1)} fusion(f32[16,512,1024]{2,1,0:T(8,128)} %get-tuple-element.496, f32[16,512]{1,0:T(8,128)S(1)} %get-tuple-element.497, pred[512,1024]{1,0:T(8,128)(4,1)S(1)} %fusion.191), kind=kLoop, calls=%fused_computation.6.clone.1 | loop fusion | flops 33546240 | bytes 34144256 | tf_op jit(solution)/shard_map/while/body/eval_jaxpr/reduce_sum | solution.py:598
  254.8 15.0 %fusion.194 = bf16[2,1,512,16,64]{2,4,3,1,0:T(8,128)(2,1)S(1)} fusion(bf16[2,1,512,16,64]{2,4,3,1,0:T(8,128)(2,1)S(1)} %get-tuple-element.523, s32[]{:T(128)S(6)} %copy.249, bf16[1,1024,16,64]{1,3,2,0:T(8,128)(2,1)} %get-tuple-element.540, f32[16,512,1024]{2,1,0:T(8,128)} %get-tuple-element.496, f32[16,512]{1,0:T(8,128)S(1)} %fusion.193, ...), kind=kOutput, calls=%fused_computation.15.clone.1 | convolution fusion | flops 1116209152 | bytes 37289988 | tf_op jit(solution)/shard_map/while/body/eval_jaxpr/bhqk,bkhd->bqhd/dot_general | solution.py:600
  273.6 16.5 %fusion.192 = (f32[16,512]{1,0:T(8,128)S(1)}, f32[16,512,1024]{2,1,0:T(8,128)}) fusion(pred[512,1024]{1,0:T(8,128)(4,1)S(1)} %fusion.191, bf16[1,1024,16,64]{1,3,2,0:T(8,128)(2,1)} %get-tuple-element.539, bf16[1,1024,16,64]{1,3,2,0:T(8,128)(2,1)} %get-tuple-element.538, s32[]{:T(128)S(6)} %select_n.59), kind=kOutput, calls=%fused_computation.5.clone.1 | convolution fusion | flops 1098899456 | bytes 37257220 | tf_op jit(solution)/shard_map/while/body/eval_jaxpr/bqhd,bkhd->bhqk/dot_general | solution.py:585
  290.1 14.9 %fusion.193 = f32[16,512]{1,0:T(8,128)S(1)} fusion(f32[16,512,1024]{2,1,0:T(8,128)} %get-tuple-element.496, f32[16,512]{1,0:T(8,128)S(1)} %get-tuple-element.497, pred[512,1024]{1,0:T(8,128)(4,1)S(1)} %fusion.191), kind=kLoop, calls=%fused_computation.6.clone.1 | loop fusion | flops 33546240 | bytes 34144256 | tf_op jit(solution)/shard_map/while/body/eval_jaxpr/reduce_sum | solution.py:598
  305.0 15.0 %fusion.194 = bf16[2,1,512,16,64]{2,4,3,1,0:T(8,128)(2,1)S(1)} fusion(bf16[2,1,512,16,64]{2,4,3,1,0:T(8,128)(2,1)S(1)} %get-tuple-element.523, s32[]{:T(128)S(6)} %copy.249, bf16[1,1024,16,64]{1,3,2,0:T(8,128)(2,1)} %get-tuple-element.540, f32[16,512,1024]{2,1,0:T(8,128)} %get-tuple-element.496, f32[16,512]{1,0:T(8,128)S(1)} %fusion.193, ...), kind=kOutput, calls=%fused_computation.15.clone.1 | convolution fusion | flops 1116209152 | bytes 37289988 | tf_op jit(solution)/shard_map/while/body/eval_jaxpr/bhqk,bkhd->bqhd/dot_general | solution.py:600
  328.3 9.4 fusion.108
  337.7 9.4 fusion.107
  347.1 22.0 %fusion.57 = (bf16[1024,2816]{1,0:T(8,128)(2,1)}, bf16[1024,2816]{1,0:T(8,128)(2,1)}, bf16[1024,2816]{1,0:T(8,128)(2,1)}) fusion(f32[1024,2816]{1,0:T(8,128)} %fusion.107, f32[1024,2816]{1,0:T(8,128)} %fusion.108, bf16[2816,1024]{1,0:T(8,128)(2,1)} %bitcast.389, bf16[1,1024,1024]{2,1,0:T(8,128)(2,1)S(1)} %copy-done.30), kind=kOutput, calls=%fused_computation.63 | convolution fusion | flops 5948833792 | bytes 48234496 | tf_op jit(solution)/shard_map/dot_general | solution.py:80
  369.1 11.7 %fusion.79 = bf16[1,1024,1024]{1,2,0:T(8,128)(2,1)} fusion(f32[1024,1024]{0,1:T(8,128)} %copy-done.9, bf16[1024,2816]{1,0:T(8,128)(2,1)} %get-tuple-element.356, bf16[2816,1024]{1,0:T(8,128)(2,1)} %bitcast.390), kind=kOutput, calls=%fused_computation.102 | convolution fusion | flops 5907677184 | bytes 17825792 | tf_op jit(solution)/shard_map/dot_general | solution.py:70
  380.8 10.0 %fusion.109 = f32[1024,1024]{0,1:T(8,128)S(1)} fusion(bf16[1024,2816]{1,0:T(8,128)(2,1)} %get-tuple-element.355, bf16[1024,2816]{1,0:T(8,128)(2,1)} %bitcast.385), kind=kOutput, calls=%fused_computation.182 | convolution fusion | flops 5905580032 | bytes 15728640 | tf_op jit(solution)/shard_map/dot_general | solution.py:80
  390.9 8.9 multiply_reduce_fusion.1
  399.7 8.1 convolution_convert_fusion.1
  407.9 10.6 %convolution_convert_fusion.2 = bf16[1024,2816]{1,0:T(8,128)(2,1)} fusion(bf16[1024,1024]{0,1:T(8,128)(2,1)S(1)} %copy-done.36, bf16[1024,2816]{1,0:T(8,128)(2,1)} %get-tuple-element.355), kind=kOutput, calls=%fused_computation.72 | convolution fusion | flops 5908463616 | bytes 13631488 | tf_op jit(solution)/shard_map/dot_general | solution.py:74
  422.5 4.6 multiply_subtract_fusion
  434.6 229.4 %while.29 = (s32[]{:T(128)}, f32[1,1024,16,64]{1,3,2,0:T(8,128)}, f32[1,1024,16,64]{1,3,2,0:T(8,128)}, f32[2,1,512,16,64]{2,4,3,1,0:T(8,128)}, s32[2]{0:T(128)S(...) while((s32[]{:T(128)}, f32[1,1024,16,64]{1,3,2,0:T(8,128)}, ...), condition=%wide.region_9.10_spmd.clone, body=%wide.region_7.9_spmd.clone.sunk | while | flops 5501870592 | bytes 350468352 | solution.py:669
  438.7 17.7 %fusion.203 = f32[16,512,1024]{2,1,0:T(8,128)} fusion(bf16[1,1024,16,64]{1,3,2,0:T(8,128)(2,1)} %get-tuple-element.579, bf16[1,1024,16,64]{1,3,2,0:T(8,128)(2,1)} %get-tuple-element.577, s32[]{:T(128)S(6)} %select_n.63), kind=kOutput, calls=%fused_computation.37.clone.1 | convolution fusion | flops 1073741824 | bytes 36700164 | tf_op jit(solution)/shard_map/while/body/eval_jaxpr/bqhd,bkhd->bhqk/dot_general | solution.py:585
  456.4 17.8 %bitcast_add_fusion.5 = f32[1,1024,16,64]{1,3,2,0:T(8,128)} fusion(f32[1,1024,16,64]{1,3,2,0:T(8,128)} %get-tuple-element.560, f32[16,512,1024]{2,1,0:T(8,128)} %fusion.203, f32[16,512]{1,0:T(8,128)S(1)} %dynamic-slice_bitcast_fusion.2, pred[512,1024]{1,0:T(8,128)(4,1)S(1)} %fusion.204, pred[]{:T(512)S(6)} %compare.3, ...), kind=kOutput, calls=%fused_computation.30.clone.1 | convolution fusion | flops 1109393408 | bytes 43548676 | tf_op jit(solution)/shard_map/while/body/eval_jaxpr/bhqk,bqhd->bkhd/dot_general | solution.py:647
  474.2 26.0 %multiply_reduce_fusion.5 = (f32[16,512]{1,0:T(8,128)S(1)}, f32[16,512,1024]{2,1,0:T(8,128)}) fusion(f32[16,512,1024]{2,1,0:T(8,128)} %fusion.203, f32[16,512]{1,0:T(8,128)S(1)} %dynamic-slice_bitcast_fusion.2, pred[512,1024]{1,0:T(8,128)(4,1)S(1)} %fusion.204, bf16[1,1024,16,64]{1,3,2,0:T(8,128)(2,1)} %get-tuple-element.582, ...), kind=kOutput, calls=%fused_computation.25.clone.1 | convolution fusion | flops 1115676672 | bytes 70844416 | tf_op jit(solution)/shard_map/while/body/eval_jaxpr/bqhd,bkhd->bhqk/dot_general | solution.py:644
  500.2 27.8 %multiply_convert_fusion.11 = bf16[16,512,1024]{2,1,0:T(8,128)(2,1)} fusion(f32[16,512,1024]{2,1,0:T(8,128)} %get-tuple-element.509, f32[16,512,1024]{2,1,0:T(8,128)} %fusion.203, f32[16,512]{1,0:T(8,128)S(1)} %get-tuple-element.510, f32[16,512]{1,0:T(8,128)S(1)} %dynamic-slice_bitcast_fusion.2, pred[512,1024]{1,0:T(8,128)(4,1)S(1)} %fusion.204), kind=kLoop, calls=%fused_computation.24.clone.1 | loop fusion | flops 50331648 | bytes 84475904 | tf_op jit(solution)/shard_map/while/body/eval_jaxpr/convert_element_type | solution.py:654
  528.0 11.4 %bitcast_add_fusion.4 = f32[1,1024,16,64]{1,3,2,0:T(8,128)} fusion(f32[1,1024,16,64]{1,3,2,0:T(8,128)} %get-tuple-element.559, bf16[16,512,1024]{2,1,0:T(8,128)(2,1)} %multiply_convert_fusion.11, pred[]{:T(512)S(6)} %compare.3, bf16[1,1024,16,64]{1,3,2,0:T(8,128)(2,1)} %get-tuple-element.577, s32[]{:T(128)S(6)} %select_n.63), kind=kOutput, calls=%fused_computation.31.clone.1 | convolution fusion | flops 1076887552 | bytes 26214404 | tf_op jit(solution)/shard_map/while/body/eval_jaxpr/bhqk,bqhd->bkhd/dot_general | solution.py:661
  540.2 8.1 bitcast_dynamic-update-slice_fusion.5
  552.1 17.6 %fusion.203 = f32[16,512,1024]{2,1,0:T(8,128)} fusion(bf16[1,1024,16,64]{1,3,2,0:T(8,128)(2,1)} %get-tuple-element.579, bf16[1,1024,16,64]{1,3,2,0:T(8,128)(2,1)} %get-tuple-element.577, s32[]{:T(128)S(6)} %select_n.63), kind=kOutput, calls=%fused_computation.37.clone.1 | convolution fusion | flops 1073741824 | bytes 36700164 | tf_op jit(solution)/shard_map/while/body/eval_jaxpr/bqhd,bkhd->bhqk/dot_general | solution.py:585
  569.7 18.9 %bitcast_add_fusion.5 = f32[1,1024,16,64]{1,3,2,0:T(8,128)} fusion(f32[1,1024,16,64]{1,3,2,0:T(8,128)} %get-tuple-element.560, f32[16,512,1024]{2,1,0:T(8,128)} %fusion.203, f32[16,512]{1,0:T(8,128)S(1)} %dynamic-slice_bitcast_fusion.2, pred[512,1024]{1,0:T(8,128)(4,1)S(1)} %fusion.204, pred[]{:T(512)S(6)} %compare.3, ...), kind=kOutput, calls=%fused_computation.30.clone.1 | convolution fusion | flops 1109393408 | bytes 43548676 | tf_op jit(solution)/shard_map/while/body/eval_jaxpr/bhqk,bqhd->bkhd/dot_general | solution.py:647
  588.6 26.0 %multiply_reduce_fusion.5 = (f32[16,512]{1,0:T(8,128)S(1)}, f32[16,512,1024]{2,1,0:T(8,128)}) fusion(f32[16,512,1024]{2,1,0:T(8,128)} %fusion.203, f32[16,512]{1,0:T(8,128)S(1)} %dynamic-slice_bitcast_fusion.2, pred[512,1024]{1,0:T(8,128)(4,1)S(1)} %fusion.204, bf16[1,1024,16,64]{1,3,2,0:T(8,128)(2,1)} %get-tuple-element.582, ...), kind=kOutput, calls=%fused_computation.25.clone.1 | convolution fusion | flops 1115676672 | bytes 70844416 | tf_op jit(solution)/shard_map/while/body/eval_jaxpr/bqhd,bkhd->bhqk/dot_general | solution.py:644
  614.6 27.8 %multiply_convert_fusion.11 = bf16[16,512,1024]{2,1,0:T(8,128)(2,1)} fusion(f32[16,512,1024]{2,1,0:T(8,128)} %get-tuple-element.509, f32[16,512,1024]{2,1,0:T(8,128)} %fusion.203, f32[16,512]{1,0:T(8,128)S(1)} %get-tuple-element.510, f32[16,512]{1,0:T(8,128)S(1)} %dynamic-slice_bitcast_fusion.2, pred[512,1024]{1,0:T(8,128)(4,1)S(1)} %fusion.204), kind=kLoop, calls=%fused_computation.24.clone.1 | loop fusion | flops 50331648 | bytes 84475904 | tf_op jit(solution)/shard_map/while/body/eval_jaxpr/convert_element_type | solution.py:654
  642.4 12.5 %bitcast_add_fusion.4 = f32[1,1024,16,64]{1,3,2,0:T(8,128)} fusion(f32[1,1024,16,64]{1,3,2,0:T(8,128)} %get-tuple-element.559, bf16[16,512,1024]{2,1,0:T(8,128)(2,1)} %multiply_convert_fusion.11, pred[]{:T(512)S(6)} %compare.3, bf16[1,1024,16,64]{1,3,2,0:T(8,128)(2,1)} %get-tuple-element.577, s32[]{:T(128)S(6)} %select_n.63), kind=kOutput, calls=%fused_computation.31.clone.1 | convolution fusion | flops 1076887552 | bytes 26214404 | tf_op jit(solution)/shard_map/while/body/eval_jaxpr/bhqk,bqhd->bkhd/dot_general | solution.py:661
  655.6 8.1 bitcast_dynamic-update-slice_fusion.5
  665.1 8.2 copy.194
  673.3 9.7 %fusion.113 = f32[1024,2,64]{2,1,0:T(2,128)S(1)} fusion(f32[1024,2,16]{2,1,0:T(2,128)S(1)} %copy-done.20, f32[1024,16,64]{2,1,0:T(8,128)} %copy.194), kind=kOutput, calls=%fused_computation.186 | convolution fusion | flops 25165824 | bytes 4849664 | tf_op jit(solution)/shard_map/bshd,bsrh->bsrd/dot_general | solution.py:91
  683.1 14.2 %fusion.112 = f32[1024,2,16]{2,1,0:T(2,128)} fusion(f32[1024,2,64]{2,1,0:T(2,128)S(1)} %copy-done.18, f32[1024,16,64]{2,1,0:T(8,128)S(1)} %copy-done.1), kind=kOutput, calls=%fused_computation.185 | convolution fusion | flops 25165824 | bytes 4849664 | tf_op jit(solution)/shard_map/bshd,bsrd->bsrh/dot_general | solution.py:90
  706.6 8.3 copy.236
  714.9 13.3 %fusion.111 = f32[1024,6,64]{2,1,0:T(8,128)} fusion(f32[1024,6,16]{2,1,0:T(8,128)} %copy.157, f32[1024,16,64]{2,1,0:T(8,128)} %bitcast.327), kind=kOutput, calls=%fused_computation.184 | convolution fusion | flops 75497472 | bytes 6160384 | tf_op jit(solution)/shard_map/bshd,bsrh->bsrd/dot_general | solution.py:91
  728.2 14.7 %fusion.110 = f32[1024,6,16]{2,1,0:T(8,128)} fusion(f32[1024,6,64]{2,1,0:T(8,128)S(1)} %copy-done.4, f32[1024,16,64]{2,1,0:T(8,128)S(1)} %bitcast.328), kind=kOutput, calls=%fused_computation.183 | convolution fusion | flops 75497472 | bytes 6160384 | tf_op jit(solution)/shard_map/bshd,bsrd->bsrh/dot_general | solution.py:90
  760.9 8.1 convolution_convert_fusion
  769.0 8.2 copy.202
  777.2 9.7 %fusion.115 = f32[1024,2,64]{2,1,0:T(2,128)S(1)} fusion(f32[1024,2,16]{2,1,0:T(2,128)S(1)} %copy-done.16, f32[1024,16,64]{2,1,0:T(8,128)} %copy.202), kind=kOutput, calls=%fused_computation.188 | convolution fusion | flops 25165824 | bytes 4849664 | tf_op jit(solution)/shard_map/bshd,bsrh->bsrd/dot_general | solution.py:91
  786.9 13.5 %fusion.114 = f32[1024,2,16]{2,1,0:T(2,128)S(1)} fusion(f32[1024,2,64]{2,1,0:T(2,128)S(1)} %copy-done.14, f32[1024,16,64]{2,1,0:T(8,128)S(1)} %copy-done.2), kind=kOutput, calls=%fused_computation.187 | convolution fusion | flops 25165824 | bytes 4849664 | tf_op jit(solution)/shard_map/bshd,bsrd->bsrh/dot_general | solution.py:90
  806.6 6.1 fusion.73
  821.9 134.6 %scatter_gradients.1 = (f32[32,2816]{1,0:T(8,128)}, f32[32,2816]{1,0:T(8,128)}, f32[88,1024]{1,0:T(8,128)}, f32[32,1024]{1,0:T(8,128)}, f32[32,896]{1,0:T(8,128)}) custom-call(bf16[2,2,4,2,32,2816]{5,4,3,2,1,0:T(8,128)(2,1)} %bitcast.344, bf16[2,2,4,2,32,2816]{5,4,3,2,1,0:T(8,128)(2,1)} %bitcast.343, bf16[2,2,4,2,88,1024]{5,4,3,2,1,0:T(8,128)(2,1)} %bitcast.345, ...), custom_call_target="tpu_custom_call" | custom-call | tf_op jit(solution)/shard_map/scatter_gradients/pallas_call | solution.py:504
  (277 shorter events, 125.5 us)
Async XLA Ops:
  4.9 140.3 %copy-start.24 = (f32[1024,32]{0,1:T(8,128)}, f32[1024,32]{0,1:T(8,128)S(1)}, u32[]{:S(2)}) copy-start(f32[1024,32]{0,1:T(8,128)S(1)} %get-tuple-element.381) | copy-start | bytes 393220
  4.9 140.3 %copy-start.26 = (f32[1024,32]{0,1:T(8,128)}, f32[1024,32]{0,1:T(8,128)S(1)}, u32[]{:S(2)}) copy-start(f32[1024,32]{0,1:T(8,128)S(1)} %get-tuple-element.382) | copy-start | bytes 393220
  7.9 130.8 %copy-start.5 = (bf16[1,1024,1024]{1,2,0:T(8,128)(2,1)}, bf16[1,1024,1024]{1,2,0:T(8,128)(2,1)S(1)}, u32[]{:S(2)}) copy-start(bf16[1,1024,1024]{1,2,0:T(8,128)(2,1)S(1)} %copy.149) | copy-start | bytes 6291460
  9.2 129.5 %copy-start.55 = (f32[1024]{0:T(1024)}, f32[1024]{0:T(1024)S(1)}, u32[]{:S(2)}) copy-start(f32[1024]{0:T(1024)S(1)} %get-tuple-element.378) | copy-start | bytes 12292
  145.9 52.7 %copy-start.17 = (f32[1024,2,64]{2,1,0:T(2,128)}, f32[1024,2,64]{2,1,0:T(2,128)S(1)}, u32[]{:S(2)}) copy-start(f32[1024,2,64]{2,1,0:T(2,128)S(1)} %copy.164) | copy-start | bytes 1572868
  146.4 31.7 %copy-start.13 = (f32[1024,2,64]{2,1,0:T(2,128)}, f32[1024,2,64]{2,1,0:T(2,128)S(1)}, u32[]{:S(2)}) copy-start(f32[1024,2,64]{2,1,0:T(2,128)S(1)} %copy.170) | copy-start | bytes 1572868
  148.3 29.8 %copy-start.15 = (f32[1024,2,16]{2,1,0:T(2,128)}, f32[1024,2,16]{2,1,0:T(2,128)S(1)}, u32[]{:S(2)}) copy-start(f32[1024,2,16]{2,1,0:T(2,128)S(1)} %copy.169) | copy-start | bytes 393220
  192.9 5.6 copy-start.19
  213.7 5.6 copy-start.32
  213.8 5.6 copy-start.38
  323.1 5.2 slice-start
  327.9 9.9 %slice-start.4 = ((s8[5767168]{0:T(1024)(128)(4,1)}), s8[4194304]{0:T(1024)(128)(4,1)S(1)}, s32[]{:S(2)}) async-start(s8[5767168]{0:T(1024)(128)(4,1)} %bitcast.386), calls=%async_computation.4 | async-start | bytes 8388608
  328.3 9.4 copy-start.35
  328.3 9.4 slice-start.5
  337.7 9.4 copy-start.30
  369.1 21.7 %slice-start.2 = ((s8[5767168]{0:T(1024)(128)(4,1)}), s8[1572864]{0:T(1024)(128)(4,1)S(1)}, s32[]{:S(2)}) async-start(s8[5767168]{0:T(1024)(128)(4,1)} %bitcast.382), calls=%async_computation.2 | async-start | bytes 3145728
  369.1 21.7 %slice-start.6 = ((s8[5767168]{0:T(1024)(128)(4,1)}), s8[4194304]{0:T(1024)(128)(4,1)S(1)}, s32[]{:S(2)}) async-start(s8[5767168]{0:T(1024)(128)(4,1)} %bitcast.393), calls=%async_computation.6 | async-start | bytes 8388608
  380.7 10.1 %copy-start.10 = (f32[1024,1024]{0,1:T(8,128)S(1)}, f32[1024,1024]{0,1:T(8,128)}, u32[]{:S(2)}) copy-start(f32[1024,1024]{0,1:T(8,128)} %copy-done.9) | copy-start | bytes 12582916
  380.7 10.1 %slice-start.3 = ((s8[5767168]{0:T(1024)(128)(4,1)}), s8[4194304]{0:T(1024)(128)(4,1)S(1)}, s32[]{:S(2)}) async-start(s8[5767168]{0:T(1024)(128)(4,1)} %bitcast.382), calls=%async_computation.3 | async-start | bytes 8388608
  380.7 10.1 %slice-start.7 = ((s8[5767168]{0:T(1024)(128)(4,1)}), s8[1572864]{0:T(1024)(128)(4,1)S(1)}, s32[]{:S(2)}) async-start(s8[5767168]{0:T(1024)(128)(4,1)} %bitcast.393), calls=%async_computation.7 | async-start | bytes 3145728
  390.9 8.9 copy-start.36
  434.5 229.4 %copy-start.60 = (bf16[1024]{0:T(1024)(128)(2,1)S(1)}, bf16[1024]{0:T(1024)(128)(2,1)}, u32[]{:S(2)}) copy-start(bf16[1024]{0:T(1024)(128)(2,1)} %get-tuple-element.306) | copy-start | bytes 6148
  528.0 12.1 %copy-start = (bf16[16,512,1024]{2,1,0:T(8,128)(2,1)S(1)}, bf16[16,512,1024]{2,1,0:T(8,128)(2,1)}, u32[]{:S(2)}) copy-start(bf16[16,512,1024]{2,1,0:T(8,128)(2,1)} %multiply_convert_fusion.11) | copy-start | bytes 50331652 | tf_op jit(solution)/shard_map/while
  642.4 13.3 %copy-start = (bf16[16,512,1024]{2,1,0:T(8,128)(2,1)S(1)}, bf16[16,512,1024]{2,1,0:T(8,128)(2,1)}, u32[]{:S(2)}) copy-start(bf16[16,512,1024]{2,1,0:T(8,128)(2,1)} %multiply_convert_fusion.11) | copy-start | bytes 50331652 | tf_op jit(solution)/shard_map/while
  665.1 8.2 copy-start.20
  673.3 9.7 %copy-start.1 = (f32[1024,16,64]{2,1,0:T(8,128)S(1)}, f32[1024,16,64]{2,1,0:T(8,128)}, u32[]{:S(2)}) copy-start(f32[1024,16,64]{2,1,0:T(8,128)} %copy.194) | copy-start | bytes 12582916
  673.3 9.7 %copy-start.18 = (f32[1024,2,64]{2,1,0:T(2,128)S(1)}, f32[1024,2,64]{2,1,0:T(2,128)}, u32[]{:S(2)}) copy-start(f32[1024,2,64]{2,1,0:T(2,128)} %copy-done.17) | copy-start | bytes 1572868
  683.1 18.0 %copy-start.25 = (f32[1024,32]{0,1:T(8,128)S(1)}, f32[1024,32]{0,1:T(8,128)}, u32[]{:S(2)}) copy-start(f32[1024,32]{0,1:T(8,128)} %copy-done.24) | copy-start | bytes 393220
  683.1 18.0 %copy-start.27 = (f32[1024,32]{0,1:T(8,128)S(1)}, f32[1024,32]{0,1:T(8,128)}, u32[]{:S(2)}) copy-start(f32[1024,32]{0,1:T(8,128)} %copy-done.26) | copy-start | bytes 393220
  699.9 6.6 copy-start.41
  701.2 5.4 copy-start.28
  714.9 13.3 %copy-start.3 = (f32[2,1,512,16,64]{4,3,2,0,1:T(8,128)S(1)}, f32[2,1,512,16,64]{4,3,2,0,1:T(8,128)}, u32[]{:S(2)}) copy-start(f32[2,1,512,16,64]{4,3,2,0,1:T(8,128)} %copy.236) | copy-start | bytes 12582916
  714.9 13.3 %copy-start.4 = (f32[1024,6,64]{2,1,0:T(8,128)S(1)}, f32[1024,6,64]{2,1,0:T(8,128)}, u32[]{:S(2)}) copy-start(f32[1024,6,64]{2,1,0:T(8,128)} %copy.158) | copy-start | bytes 4718596
  752.6 8.2 slice-start.8
  754.9 5.9 slice-start.9
  769.0 8.2 copy-start.16
  777.2 9.7 %copy-start.2 = (f32[1024,16,64]{2,1,0:T(8,128)S(1)}, f32[1024,16,64]{2,1,0:T(8,128)}, u32[]{:S(2)}) copy-start(f32[1024,16,64]{2,1,0:T(8,128)} %copy.202) | copy-start | bytes 12582916
  777.2 9.7 %copy-start.14 = (f32[1024,2,64]{2,1,0:T(2,128)S(1)}, f32[1024,2,64]{2,1,0:T(2,128)}, u32[]{:S(2)}) copy-start(f32[1024,2,64]{2,1,0:T(2,128)} %copy-done.13) | copy-start | bytes 1572868
  800.9 5.6 copy-start.7
  800.9 5.6 copy-start.54
  800.9 5.6 copy-start.56
  806.6 6.1 copy-start.12
  806.6 6.1 copy-start.58
  821.9 141.9 %copy-start.23 = (bf16[1,1024,1024]{1,2,0:T(8,128)(2,1)S(1)}, bf16[1,1024,1024]{1,2,0:T(8,128)(2,1)}, u32[]{:S(2)}) copy-start(bf16[1,1024,1024]{1,2,0:T(8,128)(2,1)} %get-tuple-element.358) | copy-start | bytes 6291460
  956.5 9.8 %copy-start.52 = (f32[32,1024]{1,0:T(8,128)S(1)}, f32[32,1024]{1,0:T(8,128)}, u32[]{:S(2)}) copy-start(f32[32,1024]{1,0:T(8,128)} %get-tuple-element.609) | copy-start | bytes 393220
  956.5 10.5 %copy-start.47 = (f32[32,2816]{1,0:T(8,128)S(1)}, f32[32,2816]{1,0:T(8,128)}, u32[]{:S(2)}) copy-start(f32[32,2816]{1,0:T(8,128)} %get-tuple-element.611) | copy-start | bytes 1081348
  956.5 11.2 %copy-start.46 = (f32[32,2816]{1,0:T(8,128)S(1)}, f32[32,2816]{1,0:T(8,128)}, u32[]{:S(2)}) copy-start(f32[32,2816]{1,0:T(8,128)} %get-tuple-element.612) | copy-start | bytes 1081348
  956.5 11.9 %copy-start.45 = (f32[88,1024]{1,0:T(8,128)S(1)}, f32[88,1024]{1,0:T(8,128)}, u32[]{:S(2)}) copy-start(f32[88,1024]{1,0:T(8,128)} %get-tuple-element.613) | copy-start | bytes 1081348
  (28 other events, 87.6 us)

commit v2 on v1

--- a/solution.py
+++ b/solution.py
@@ -3,93 +3,287 @@
 
 import jax
 import jax.numpy as jnp
+import numpy as np
 from jax import lax
 from jax.experimental import pallas as pl
 from jax.experimental.pallas import tpu as pltpu
 from jax.sharding import PartitionSpec as P
 
 MESH = pl.DeviceIdType.MESH
-
-D = 1024
-H = 16
-DH = 64
-RQ = 6
-RK = 2
+D, H, DH, RQ, RK = 1024, 16, 64, 6, 2
 PACKED = 896
-
-
+DIMS, HEADS = 640, 128
+BLOCK = 256
+BACK = 512
+NEG = -1e30
 epsilon = 1e-06
 theta_base = 10000.0
-highest = lax.Precision.HIGHEST
-
-
-def rotary_tables(seq_len, half_dim):
-    position = jnp.arange(seq_len, dtype=jnp.float32)
-    inverse = jnp.exp(
-        -math.log(theta_base) * 2.0 * jnp.arange(half_dim, dtype=jnp.float32) / (2.0 * half_dim)
-    )
-    angle = position[:, None] * inverse[None, :]
-    return (jnp.cos(angle), jnp.sin(angle))
-
-
-def rotate(factor, cosine_table, sine_table):
-    half_dim = factor.shape[-1] // 2
-    first_half = factor[..., :half_dim]
-    second_half = factor[..., half_dim:]
-    cosine_part = cosine_table[:, None, :]
-    sine_part = sine_table[:, None, :]
-    return jnp.concatenate(
-        [
-            first_half * cosine_part - second_half * sine_part,
-            first_half * sine_part + second_half * cosine_part,
+f32, bf16 = jnp.float32, jnp.bfloat16
+NT = (((1,), (1,)), ((), ()))
+NN = (((1,), (0,)), ((), ()))
+TN = (((0,), (0,)), ((), ()))
+
+
+def dot(a, b, dims=NN):
+    return lax.dot_general(a, b, dims, preferred_element_type=f32)
+
+
+def params(**kw):
+    return pltpu.CompilerParams(vmem_limit_bytes=56 << 20, **kw)
+
+
+def rope_tables(seq_len):
+    half = DH // 2
+    position = np.arange(seq_len, dtype=np.float32)
+    inverse = np.exp(-math.log(theta_base) * 2.0 * np.arange(half, dtype=np.float32) / np.float32(2.0 * half)).astype(np.float32)
+    angle = (position[:, None] * inverse[None, :]).astype(np.float32)
+    cosine, sine = np.cos(angle), np.sin(angle)
+    return (np.concatenate([cosine] * 4, 1), np.concatenate([-sine, sine] * 2, 1))
+
+
+def spread_table():
+    out = np.zeros((8, 2 * HEADS, H * DH), np.float32)
+    for j in range(8):
+        for h in range(H):
+            out[j, [j * H + h, HEADS + j * H + h], h * DH:(h + 1) * DH] = 1.0
+    return out.astype(jnp.bfloat16)
+
+
+def low_lane(shape):
+    return lax.rem(lax.broadcasted_iota(jnp.int32, shape, 1), 128) < 64
+
+
+def first_half(shape):
+    return lax.rem(lax.broadcasted_iota(jnp.int32, shape, 1), 64) < 32
+
+
+def turn(x, cosine, sine):
+    partner = jnp.where(first_half(x.shape), pltpu.roll(x, 96, 1), pltpu.roll(x, 32, 1))
+    return x * cosine + partner * sine
+
+
+def split_bf16(x):
+    hi = x.astype(bf16)
+    return jnp.concatenate([hi, (x - hi.astype(f32)).astype(bf16)], axis=1)
+
+
+def twice(x, rank):
+    rolled = pltpu.roll(x, 64, 1)
+    low = low_lane(x.shape)
+    return jnp.where(low, x, rolled) if rank % 2 == 0 else jnp.where(low, rolled, x)
+
+
+def wide(x):
+    return jnp.concatenate([x] * (H * DH // 128), axis=1)
+
+
+def rms(x):
+    return lax.rsqrt(jnp.mean(x * x, axis=-1, keepdims=True) + epsilon)
+
+
+FACTORS = ((0, RQ, 0), (RQ, RK, 3), (0, RK, 4))
+
+
+def factors_kernel(tokens, gain, weight, cosine, sine, spread, normed, factors, query, key, value):
+    x = tokens[...].astype(f32)
+    n = (x * rms(x) * gain[...]).astype(bf16)
+    normed[...] = n
+    f = dot(n, weight[...])
+    pairs = [f[:, 128 * i:128 * i + 128] for i in range(DIMS // 128)]
+    pairs = [turn(p, cosine[...], sine[...]) if i < 4 else p for i, p in enumerate(pairs)]
+    for i, p in enumerate(pairs):
+        factors[:, 128 * i:128 * i + 128] = p
+    factors[:, DIMS:] = f[:, DIMS:]
+    heads_qk = split_bf16(f[:, DIMS:DIMS + HEADS])
+    heads_v = split_bf16(f[:, DIMS + HEADS:])
+    for out, heads, (at, ranks, pair), scale in zip(
+        (query, key, value), (heads_qk, heads_qk, heads_v), FACTORS, (0.125, 1.0, 1.0)
+    ):
+        total = None
+        for r in range(ranks):
+            term = dot(heads, spread[at + r]) * wide(twice(pairs[pair + r // 2], r))
+            total = term if total is None else total + term
+        rounded = (total * (1.0 / ranks)).astype(bf16)
+        out[...] = rounded * jnp.asarray(scale, bf16) if scale != 1.0 else rounded
+
+
+def make_factors(tokens, gain, weight, tables):
+    cosine, sine, spread = tables
+    seq = tokens.shape[0]
+    row = lambda width: pl.BlockSpec((BLOCK, width), lambda i: (i, 0))
+    whole = lambda a: pl.BlockSpec(a.shape, lambda i: (0,) * a.ndim)
+    return pl.pallas_call(
+        factors_kernel,
+        grid=(seq // BLOCK,),
+        out_shape=[
+            jax.ShapeDtypeStruct((seq, D), bf16),
+            jax.ShapeDtypeStruct((seq, PACKED), f32),
+        ] + [jax.ShapeDtypeStruct((seq, H * DH), bf16)] * 3,
+        in_specs=[row(D), whole(gain), whole(weight), row(128), row(128), whole(spread)],
+        out_specs=[row(D), row(PACKED)] + [row(H * DH)] * 3,
+        compiler_params=params(),
+        name="factors",
+    )(tokens, gain, weight, cosine, sine, spread)
+
+
+def allowed_t(doc_col, doc_row, k0, kn, q0, qn):
+    same = doc_col[k0:k0 + kn, :] == doc_row[:, q0:q0 + qn]
+    if k0 + kn - 1 > q0:
+        k_at = k0 + lax.broadcasted_iota(jnp.int32, (kn, qn), 0)
+        q_at = q0 + lax.broadcasted_iota(jnp.int32, (kn, qn), 1)
+        same = same & (k_at <= q_at)
+    return same
+
+
+def halves(x):
+    low = low_lane(x.shape)
+    zero = jnp.zeros_like(x)
+    return jnp.where(low, x, zero), jnp.where(low, zero, x)
+
+
+def attend_kernel(doc_col, doc_row, query, key, value, mixed, lse):
+    seq = query.shape[0]
+    v_half = halves(value[...])
+    for q0 in range(0, seq, BLOCK):
+        lo = max(0, q0 - BACK)
+        kn = q0 + BLOCK - lo
+        ok = allowed_t(doc_col, doc_row, lo, kn, q0, BLOCK)
+        probs = []
+        for h, q in enumerate(halves(query[q0:q0 + BLOCK, :])):
+            s = jnp.where(ok, dot(key[lo:lo + kn, :], q, NT), NEG)
+            top = jnp.max(s, axis=0, keepdims=True)
+            e = jnp.exp(s - top)
+            total = jnp.sum(e, axis=0, keepdims=True)
+            probs.append((e * (1.0 / total)).astype(bf16))
+            lse[0, h:h + 1, q0:q0 + BLOCK] = top + jnp.log(total)
+        values = jnp.concatenate([v[lo:lo + kn] for v in v_half], axis=0)
+        mixed[q0:q0 + BLOCK, :] = dot(jnp.concatenate(probs, axis=0), values, TN).astype(bf16)
+
+
+def attend(doc_col, doc_row, query, key, value):
+    seq = query.shape[0]
+    pairs = H // 2
+    whole = lambda a: pl.BlockSpec(a.shape, lambda i: (0,) * a.ndim)
+    pair = pl.BlockSpec((seq, 128), lambda i: (0, i))
+    return pl.pallas_call(
+        attend_kernel,
+        grid=(pairs,),
+        out_shape=[jax.ShapeDtypeStruct((seq, H * DH), bf16), jax.ShapeDtypeStruct((pairs, 2, seq), f32)],
+        in_specs=[whole(doc_col), whole(doc_row), pair, pair, pair],
+        out_specs=[pair, pl.BlockSpec((1, 2, seq), lambda i: (i, 0, 0))],
+        compiler_params=params(),
+        name="attend",
+    )(doc_col, doc_row, query, key, value)
+
+
+def attend_back_kernel(doc_col, doc_row, query, key, value, grad, lse, g_query, g_key, g_value):
+    seq = query.shape[0]
+    k_half = halves(key[...])
+    for q0 in range(0, seq, BLOCK):
+        lo = max(0, q0 - BACK)
+        kn = q0 + BLOCK - lo
+        ok = allowed_t(doc_col, doc_row, lo, kn, q0, BLOCK)
+        ps, ds = [], []
+        q_half, g_half = halves(query[q0:q0 + BLOCK, :]), halves(grad[q0:q0 + BLOCK, :])
+        for h in (0, 1):
+            s = dot(key[lo:lo + kn, :], q_half[h], NT)
+            p = jnp.where(ok, jnp.exp(s - lse[0, h:h + 1, q0:q0 + BLOCK]), 0.0)
+            pd = p * dot(value[lo:lo + kn, :], g_half[h], NT)
+            ps.append(p.astype(bf16))
+            ds.append((pd - p * jnp.sum(pd, axis=0, keepdims=True)).astype(bf16))
+        to_value = dot(jnp.concatenate(ps, 1), jnp.concatenate(g_half, 0))
+        to_key = dot(jnp.concatenate(ds, 1), jnp.concatenate(q_half, 0))
+        if q0 > lo:
+            g_value[lo:q0, :] += to_value[:q0 - lo]
+            g_key[lo:q0, :] += to_key[:q0 - lo]
+        g_value[q0:q0 + BLOCK, :] = to_value[q0 - lo:]
+        g_key[q0:q0 + BLOCK, :] = to_key[q0 - lo:]
+        keys = jnp.concatenate([k[lo:lo + kn] for k in k_half], 0)
+        g_query[q0:q0 + BLOCK, :] = dot(jnp.concatenate(ds, 0), keys, TN) * 0.125
+
+
+def attend_back(doc_col, doc_row, query, key, value, grad, lse):
+    seq = query.shape[0]
+    pairs = H // 2
+    whole = lambda a: pl.BlockSpec(a.shape, lambda i: (0,) * a.ndim)
+    pair = pl.BlockSpec((seq, 128), lambda i: (0, i))
+    return pl.pallas_call(
+        attend_back_kernel,
+        grid=(pairs,),
+        out_shape=[jax.ShapeDtypeStruct((seq, H * DH), f32)] * 3,
+        in_specs=[whole(doc_col), whole(doc_row)] + [pair] * 4 + [pl.BlockSpec((1, 2, seq), lambda i: (i, 0, 0))],
+        out_specs=[pair] * 3,
+        compiler_params=params(),
+        name="attend_back",
+    )(doc_col, doc_row, query, key, value, grad, lse)
+
+
+def factors_back_kernel(tokens, gain, weight, cosine, sine, spread, factors, g_query, g_key, g_value, g_middle,
+                        g_factors, g_tokens, g_gain):
+    pairs = [factors[:, 128 * i:128 * i + 128] for i in range(DIMS // 128)]
+    heads_qk = split_bf16(factors[:, DIMS:DIMS + HEADS])
+    heads_v = split_bf16(factors[:, DIMS + HEADS:])
+    g_heads = [None, None]
+    for grad, heads, which, (at, ranks, pair) in zip(
+        (g_query, g_key, g_value), (heads_qk, heads_qk, heads_v), (0, 0, 1), FACTORS
+    ):
+        g = grad[...] * (1.0 / ranks)
+        folded = []
+        for r in range(ranks):
+            product = (g * wide(twice(pairs[pair + r // 2], r))).astype(bf16)
+            part = dot(product, spread[at + r, :HEADS, :], NT)
+            g_heads[which] = part if g_heads[which] is None else g_heads[which] + part
+            full = g * dot(heads, spread[at + r])
+            folded.append(sum(full[:, 128 * i:128 * i + 128] for i in range(H * DH // 128)))
+        for r in range(0, ranks, 2):
+            a, b = folded[r], folded[r + 1]
+            low = low_lane(a.shape)
+            mine = jnp.where(low, a, b)
+            other = jnp.where(low, pltpu.roll(a, 64, 1), pltpu.roll(b, 64, 1))
+            both = mine + other
+            i = pair + r // 2
+            if i < 4:
+                both = turn(both, cosine[...], -sine[...])
+            g_factors[:, 128 * i:128 * i + 128] = both.astype(bf16)
+    g_factors[:, DIMS:DIMS + HEADS] = g_heads[0].astype(bf16)
+    g_factors[:, DIMS + HEADS:] = g_heads[1].astype(bf16)
+    g_normed = dot(g_factors[...], weight[...], NT)
+    x = tokens[...].astype(f32)
+    r1 = rms(x)
+    u = g_normed * gain[...]
+    part = jnp.sum(g_normed * x * r1, axis=0, keepdims=True)
+
+    @pl.when(pl.program_id(0) == 0)
+    def _():
+        g_gain[...] = part
+
+    @pl.when(pl.program_id(0) > 0)
+    def _():
+        g_gain[...] += part
+
+    g_tokens[...] = (g_middle[...] + r1 * u - x * (r1 * r1 * r1 * jnp.mean(u * x, axis=-1, keepdims=True))).astype(bf16)
+
+
+def factors_back(tokens, gain, weight, tables, factors, g_query, g_key, g_value, g_middle):
+    cosine, sine, spread = tables
+    seq = tokens.shape[0]
+    row = lambda width: pl.BlockSpec((BLOCK, width), lambda i: (i, 0))
+    whole = lambda a: pl.BlockSpec(a.shape, lambda i: (0,) * a.ndim)
+    return pl.pallas_call(
+        factors_back_kernel,
+        grid=(seq // BLOCK,),
+        out_shape=[
+            jax.ShapeDtypeStruct((seq, PACKED), bf16),
+            jax.ShapeDtypeStruct((seq, D), bf16),
+            jax.ShapeDtypeStruct((1, D), f32),
         ],
-        axis=-1,
-    )
-
-
-def rotate_back(grad_factor, cosine_table, sine_table):
-    half_dim = grad_factor.shape[-1] // 2
-    first_half = grad_factor[..., :half_dim]
-    second_half = grad_factor[..., half_dim:]
-    cosine_part = cosine_table[:, None, :]
-    sine_part = sine_table[:, None, :]
-    return jnp.concatenate(
-        [
-            first_half * cosine_part + second_half * sine_part,
-            second_half * cosine_part - first_half * sine_part,
-        ],
-        axis=-1,
-    )
-
-
-def rms_scale(values):
-    return lax.rsqrt(jnp.mean(values * values, axis=-1, keepdims=True) + epsilon)
-
-
-def forward_dot(left, right):
-    return jnp.dot(left, right, preferred_element_type=jnp.float32)
-
-
-def outer_sum(left, right):
-    return lax.dot_general(
-        left, right, (((0,), (0,)), ((), ())), preferred_element_type=jnp.float32
-    )
-
-
-def back_dot(grad_rows, weight):
-    return lax.dot_general(
-        grad_rows, weight, (((1,), (1,)), ((), ())), preferred_element_type=jnp.float32
-    )
-
-
-def combine_factors(heads_act, dims_act, rank_count):
-    return jnp.einsum("bsrh,bsrd->bshd", heads_act, dims_act, precision=highest) / rank_count
-
-
-def split_factors(grad_full, heads_act, dims_act, rank_count):
-    grad_heads = jnp.einsum("bshd,bsrd->bsrh", grad_full, dims_act, precision=highest) / rank_count
-    grad_dims = jnp.einsum("bshd,bsrh->bsrd", grad_full, heads_act, precision=highest) / rank_count
-    return (grad_heads, grad_dims)
+        in_specs=[row(D), whole(gain), whole(weight), row(128), row(128), whole(spread), row(PACKED)]
+        + [row(H * DH)] * 3 + [row(D)],
+        out_specs=[row(PACKED), row(D), pl.BlockSpec((1, D), lambda i: (0, 0))],
+        compiler_params=params(),
+        name="factors_back",
+    )(tokens, gain, weight, cosine, sine, spread, factors, g_query, g_key, g_value, g_middle)
+
 ANY = pl.BlockSpec(memory_space=pl.ANY)
 
 
@@ -531,199 +725,84 @@
     w_down,
     out_grad,
 ):
-    row_count = tokens.shape[0]
-    seq_len = tokens.shape[1]
-    token_count = row_count * seq_len
-    score_scale = 1.0 / math.sqrt(DH)
-    cosine_table, sine_table = rotary_tables(seq_len, DH // 2)
-    block_len = min(512, seq_len)
-    block_count = seq_len // block_len
-    positions = jnp.arange(seq_len, dtype=jnp.int32)
-    starts = jnp.arange(block_count) * block_len
-    parts = (w_query_heads, w_query_dims, w_key_heads, w_key_dims, w_value_heads, w_value_dims)
+    seq_len = tokens.shape[0] * tokens.shape[1]
+    tables = tuple(jnp.asarray(t) for t in rope_tables(seq_len) + (spread_table(),))
+    parts = (w_query_dims, w_key_dims, w_value_dims, w_query_heads, w_key_heads, w_value_heads)
     edges = [0]
     for part in parts:
         edges.append(edges[-1] + part.shape[1])
+    gains_at = edges[-1]
     packed = jnp.concatenate(
         parts
         + (norm_gain[:, None], mlp_gain[:, None])
-        + (jnp.zeros((norm_gain.shape[0], PACKED - edges[-1] - 2), jnp.bfloat16),),
+        + (jnp.zeros((norm_gain.shape[0], PACKED - gains_at - 2), bf16),),
         axis=1,
     )
     packed_w, output_w, gate_w, up_w, down_w = gather(
         dims, [packed, w_output, w_gate, w_up, w_down], 0
     )
-    query_heads_w, query_dims_w, key_heads_w, key_dims_w, value_heads_w, value_dims_w = [
-        packed_w[:, lo:hi] for lo, hi in zip(edges, edges[1:])
-    ]
-    gain_one, gain_two = packed_w[:, edges[-1]], packed_w[:, edges[-1] + 1]
-    inputs_flat = tokens.astype(jnp.float32).reshape(token_count, D)
-    scale_one = rms_scale(inputs_flat)
-    normed = (inputs_flat * scale_one * gain_one.astype(jnp.float32)).astype(jnp.bfloat16)
-    heads_query = forward_dot(normed, query_heads_w).reshape(row_count, seq_len, RQ, H)
-    dims_query = rotate(
-        forward_dot(normed, query_dims_w).reshape(row_count, seq_len, RQ, DH),
-        cosine_table,
-        sine_table,
-    )
-    heads_key = forward_dot(normed, key_heads_w).reshape(row_count, seq_len, RK, H)
-    dims_key = rotate(
-        forward_dot(normed, key_dims_w).reshape(row_count, seq_len, RK, DH),
-        cosine_table,
-        sine_table,
-    )
-    heads_value = forward_dot(normed, value_heads_w).reshape(row_count, seq_len, RK, H)
-    dims_value = forward_dot(normed, value_dims_w).reshape(row_count, seq_len, RK, DH)
-    query_full = combine_factors(heads_query, dims_query, RQ).astype(jnp.bfloat16)
-    key_full = combine_factors(heads_key, dims_key, RK).astype(jnp.bfloat16)
-    value_full = combine_factors(heads_value, dims_value, RK).astype(jnp.bfloat16)
-
-    def block_scores(block_start):
-        query_block = lax.dynamic_slice_in_dim(query_full, block_start, block_len, 1)
-        query_doc = lax.dynamic_slice_in_dim(doc_ids, block_start, block_len, 1)
-        scores = (
-            jnp.einsum("bqhd,bkhd->bhqk", query_block, key_full, preferred_element_type=jnp.float32)
-            * score_scale
-        )
-        query_pos = block_start + jnp.arange(block_len, dtype=jnp.int32)
-        allowed = (positions[None, None, :] <= query_pos[None, :, None]) & (
-            query_doc[:, :, None] == doc_ids[:, None, :]
-        )
-        return (jnp.where(allowed[:, None, :, :], scores, -1e30), query_block)
-
-    def forward_block(block_start):
-        masked, query_block = block_scores(block_start)
-        row_max = jnp.max(masked, axis=-1, keepdims=True)
-        exp_terms = jnp.exp(masked - row_max)
-        row_total = jnp.sum(exp_terms, axis=-1, keepdims=True)
-        attn_probs = (exp_terms / row_total).astype(jnp.bfloat16)
-        mixed_block = jnp.einsum(
-            "bhqk,bkhd->bqhd", attn_probs, value_full, preferred_element_type=jnp.float32
-        )
-        return (mixed_block.astype(jnp.bfloat16), (row_max + jnp.log(row_total))[..., 0])
-
-    mixed_blocks, lse_blocks = lax.map(forward_block, starts)
-    mixed_heads = jnp.moveaxis(mixed_blocks, 0, 1).reshape(token_count, H * DH)
-    middle = inputs_flat + forward_dot(mixed_heads, output_w)
-    scale_two = rms_scale(middle)
-    gain_two_f = gain_two.astype(jnp.float32)
-    normed_two = (middle * scale_two * gain_two_f).astype(jnp.bfloat16)
-    gate_proj = forward_dot(normed_two, gate_w)
-    up_proj = forward_dot(normed_two, up_w)
+    gain_one, gain_two = [packed_w[:, gains_at + i].astype(f32).reshape(1, D) for i in (0, 1)]
+
+    inputs = tokens.reshape(seq_len, D)
+    doc_row, doc_col = doc_ids.reshape(1, seq_len), doc_ids.reshape(seq_len, 1)
+    normed, factors, query, key, value = make_factors(inputs, gain_one, packed_w, tables)
+    mixed, lse = attend(doc_col, doc_row, query, key, value)
+
+    middle = inputs.astype(f32) + dot(mixed, output_w)
+    scale_two = rms(middle)
+    normed_two = (middle * scale_two * gain_two).astype(bf16)
+    gate_proj, up_proj = dot(normed_two, gate_w), dot(normed_two, up_w)
     sigmoid_gate = jax.nn.sigmoid(gate_proj)
     silu_gate = gate_proj * sigmoid_gate
-    inner_act = (silu_gate * up_proj).astype(jnp.bfloat16)
-    result = middle + forward_dot(inner_act, down_w)
-    output = result.astype(jnp.bfloat16).reshape(tokens.shape)
-    cotangent = out_grad.reshape(token_count, D)
-    grad_inner = back_dot(cotangent, down_w)
+    inner_act = (silu_gate * up_proj).astype(bf16)
+    output = (middle + dot(inner_act, down_w)).astype(bf16)
+
+    cotangent = out_grad.reshape(seq_len, D)
+    grad_inner = dot(cotangent, down_w, NT)
     grad_gate = (
         grad_inner * up_proj * sigmoid_gate * (1.0 + gate_proj * (1.0 - sigmoid_gate))
-    ).astype(jnp.bfloat16)
-    grad_up = (grad_inner * silu_gate).astype(jnp.bfloat16)
-    grad_normed_two = back_dot(grad_gate, gate_w) + back_dot(grad_up, up_w)
-    gained_two = grad_normed_two * gain_two.astype(jnp.float32)
+    ).astype(bf16)
+    grad_up = (grad_inner * silu_gate).astype(bf16)
+    grad_normed_two = dot(grad_gate, gate_w, NT) + dot(grad_up, up_w, NT)
+    gained_two = grad_normed_two * gain_two
     grad_mlp_gain = jnp.sum(grad_normed_two * middle * scale_two, axis=0)
     grad_middle = (
-        cotangent.astype(jnp.float32)
+        cotangent.astype(f32)
         + scale_two * gained_two
         - middle * scale_two**3 * jnp.mean(gained_two * middle, axis=-1, keepdims=True)
     )
-    normed_cols = normed_two
-    grad_branch = grad_middle.astype(jnp.bfloat16)
-    grad_mixed = (
-        back_dot(grad_branch, output_w).astype(jnp.bfloat16).reshape(row_count, seq_len, H, DH)
+    grad_branch = grad_middle.astype(bf16)
+    grad_mixed = dot(grad_branch, output_w, NT).astype(bf16)
+
+    grad_query, grad_key, grad_value = attend_back(
+        doc_col, doc_row, query, key, value, grad_mixed, lse
     )
-
-    def backward_block(carry_grads, block_inputs):
-        grad_key_sum, grad_value_sum = carry_grads
-        block_start, lse_block = block_inputs
-        masked, query_block = block_scores(block_start)
-        probs = jnp.exp(masked - lse_block[..., None])
-        grad_mixed_block = lax.dynamic_slice_in_dim(grad_mixed, block_start, block_len, 1)
-        grad_probs = jnp.einsum(
-            "bqhd,bkhd->bhqk", grad_mixed_block, value_full, preferred_element_type=jnp.float32
-        )
-        grad_value_sum = grad_value_sum + jnp.einsum(
-            "bhqk,bqhd->bkhd",
-            probs.astype(jnp.bfloat16),
-            grad_mixed_block,
-            preferred_element_type=jnp.float32,
-        )
-        row_delta = jnp.sum(probs * grad_probs, axis=-1, keepdims=True)
-        grad_scores = (probs * (grad_probs - row_delta)).astype(jnp.bfloat16)
-        grad_query_block = (
-            jnp.einsum("bhqk,bkhd->bqhd", grad_scores, key_full, preferred_element_type=jnp.float32)
-            * score_scale
-        )
-        grad_key_sum = (
-            grad_key_sum
-            + jnp.einsum(
-                "bhqk,bqhd->bkhd", grad_scores, query_block, preferred_element_type=jnp.float32
-            )
-            * score_scale
-        )
-        return ((grad_key_sum, grad_value_sum), grad_query_block)
-
-    zeros_full = jnp.zeros((row_count, seq_len, H, DH), jnp.float32)
-    (grad_key, grad_value), grad_query_blocks = lax.scan(
-        backward_block, (zeros_full, zeros_full), (starts, lse_blocks)
+    grad_factors, grad_tokens, grad_norm_gain = factors_back(
+        inputs, gain_one, packed_w, tables, factors, grad_query, grad_key, grad_value, grad_middle
     )
-    grad_query = jnp.moveaxis(grad_query_blocks, 0, 1).reshape(row_count, seq_len, H, DH)
-    grad_heads_query, grad_dims_query = split_factors(grad_query, heads_query, dims_query, RQ)
-    grad_heads_key, grad_dims_key = split_factors(grad_key, heads_key, dims_key, RK)
-    grad_heads_value, grad_dims_value = split_factors(grad_value, heads_value, dims_value, RK)
-    grad_dims_query = rotate_back(grad_dims_query, cosine_table, sine_table)
-    grad_dims_key = rotate_back(grad_dims_key, cosine_table, sine_table)
-    factor_pairs = (
-        (grad_heads_query, query_heads_w),
-        (grad_dims_query, query_dims_w),
-        (grad_heads_key, key_heads_w),
-        (grad_dims_key, key_dims_w),
-        (grad_heads_value, value_heads_w),
-        (grad_dims_value, value_dims_w),
-    )
-    grad_flats = []
-    grad_normed = jnp.zeros((token_count, D), jnp.float32)
-    for grad_factor, weight in factor_pairs:
-        grad_flat = grad_factor.reshape(token_count, weight.shape[1]).astype(jnp.bfloat16)
-        grad_flats.append(grad_flat)
-        grad_normed = grad_normed + back_dot(grad_flat, weight)
-    gained_one = grad_normed * gain_one.astype(jnp.float32)
-    grad_norm_gain = jnp.sum(grad_normed * inputs_flat * scale_one, axis=0)
-    grad_inputs = (
-        grad_middle
-        + scale_one * gained_one
-        - inputs_flat * scale_one**3 * jnp.mean(gained_one * inputs_flat, axis=-1, keepdims=True)
-    )
-    grad_tokens = grad_inputs.astype(jnp.bfloat16).reshape(tokens.shape)
-    normed_cols = normed
-    packed_grad = jnp.concatenate(
-        [outer_sum(normed_cols, jnp.concatenate(grad_flats, axis=1))]
-        + [grad_norm_gain[:, None], grad_mlp_gain[:, None]]
-        + [jnp.zeros((D, PACKED - edges[-1] - 2), jnp.float32)],
-        axis=1,
-    )
-    low = lambda v: v.astype(jnp.bfloat16)
+    outer_sum = lambda left, right: dot(left, right, TN).astype(bf16)
+    gains = jnp.stack([grad_norm_gain[0], grad_mlp_gain], axis=1).astype(bf16)
+    packed_grad = lax.dynamic_update_slice(outer_sum(normed, grad_factors), gains, (0, gains_at))
     gate_out, up_out, down_out, output_out, packed_out = scatter(
         dims,
         [
-            low(outer_sum(normed_two, grad_gate)),
-            low(outer_sum(normed_two, grad_up)),
-            low(outer_sum(inner_act, cotangent)),
-            low(outer_sum(mixed_heads, grad_branch)),
-            low(packed_grad),
+            outer_sum(normed_two, grad_gate),
+            outer_sum(normed_two, grad_up),
+            outer_sum(inner_act, cotangent),
+            outer_sum(mixed, grad_branch),
+            packed_grad,
         ],
         1,
     )
-    parts_out = [packed_out[:, lo:hi] for lo, hi in zip(edges, edges[1:])]
+    dims_and_heads = [packed_out[:, lo:hi] for lo, hi in zip(edges, edges[1:])]
+    grads = [g for pair in zip(dims_and_heads[3:], dims_and_heads[:3]) for g in pair]
     return (
-        output,
-        grad_tokens,
-        packed_out[:, edges[-1]],
-        *parts_out,
+        output.reshape(tokens.shape),
+        grad_tokens.reshape(tokens.shape),
+        packed_out[:, gains_at],
+        *grads,
         output_out,
-        packed_out[:, edges[-1] + 1],
+        packed_out[:, gains_at + 1],
         gate_out,
         up_out,
         down_out,
@@ -731,41 +810,11 @@
 
 
 def solution(mesh):
+    rows, matrix, vector = P(("dp", "fsdp"), None, None), P(("dp", "fsdp"), None), P(("dp", "fsdp"))
     return jax.shard_map(
         functools.partial(on_device, grid_of(mesh)),
         mesh=mesh,
-        in_specs=(
-            P(("dp", "fsdp"), None, None),
-            P(("dp", "fsdp"), None),
-            P(("dp", "fsdp")),
-            P(("dp", "fsdp"), None),
-            P(("dp", "fsdp"), None),
-            P(("dp", "fsdp"), None),
-            P(("dp", "fsdp"), None),
-            P(("dp", "fsdp"), None),
-            P(("dp", "fsdp"), None),
-            P(("dp", "fsdp"), None),
-            P(("dp", "fsdp")),
-            P(("dp", "fsdp"), None),
-            P(("dp", "fsdp"), None),
-            P(("dp", "fsdp"), None),
-            P(("dp", "fsdp"), None, None),
-        ),
-        out_specs=(
-            P(("dp", "fsdp"), None, None),
-            P(("dp", "fsdp"), None, None),
-            P(("dp", "fsdp")),
-            P(("dp", "fsdp"), None),
-            P(("dp", "fsdp"), None),
-            P(("dp", "fsdp"), None),
-            P(("dp", "fsdp"), None),
-            P(("dp", "fsdp"), None),
-            P(("dp", "fsdp"), None),
-            P(("dp", "fsdp"), None),
-            P(("dp", "fsdp")),
-            P(("dp", "fsdp"), None),
-            P(("dp", "fsdp"), None),
-            P(("dp", "fsdp"), None),
-        ),
+        in_specs=(rows, matrix, vector) + (matrix,) * 7 + (vector,) + (matrix,) * 3 + (rows,),
+        out_specs=(rows, rows, vector) + (matrix,) * 7 + (vector,) + (matrix,) * 3,
         check_vma=False,
     )

time: 979 us -> 499 us (0.51)
  matrix products: 484 us -> 115 us
  other arithmetic: 110 us -> 3.78 us
  Pallas kernels: 248 us -> 345 us
  local copies, waits for them, and re-layouts: 116 us -> 23.8 us
    dot_general x48 -> x13, matrix products: 484 us -> 115 us  [dot(): return lax.dot_general(a, b, dims, preferred_element_type=f32)]
    pallas_call x0 -> x4, Pallas kernels: none -> 95.2 us  [the longest x1 34 us: attend_back(): pl.pallas_call(attend_back_kernel, grid=(pairs,), out_shape=[jax.ShapeDty...]
    convert_element_type x10 -> x2, other arithmetic: 63 us -> 2.42 us  [the longest x1 2.01 us: on_device(): packed_w[:, gains_at + i].astype(f32).reshape(1, D)]
    unnamed x167 -> x38, local copies, waits for them, and re-layouts: 40.8 us -> 10.1 us
    reduce_sum x3 -> x0, other arithmetic: 30.3 us -> none  [the longest x2 29.8 us: forward_block(): row_total = jnp.sum(exp_terms, axis=-1, keepdims=True)]
    another operation x5 -> x2, local copies, waits for them, and re-layouts: 29.5 us -> 0.21 us  [on_device(): gains = jnp.stack([grad_norm_gain[0], grad_mlp_gain], axis=1).astype(bf16)]
    dot_general x20 -> x0, local copies, waits for them, and re-layouts: 26.2 us -> none  [the longest x14 15.5 us: forward_dot(): return jnp.dot(left, right, preferred_element_type=jnp.float32)]
where the time goes in v2:
time: 499 us; the launch traced here: 489 us
  Pallas kernels  345 us (69%)
  matrix products  115 us (23%)
  local copies, waits for them, and re-layouts  23.8 us (5%)
    pallas_call x1, Pallas kernels, scatter(): pl.pallas_call(functools.partial(scatter_kernel, dims, n), out_shape=[jax...  136 us
    dot_general x13, matrix products, dot(): return lax.dot_general(a, b, dims, preferred_element_type=f32)  115 us
    pallas_call x1, Pallas kernels, gather(): pl.pallas_call(functools.partial(gather_kernel, dims, n), out_shape=[jax....  114 us
    pallas_call x1, Pallas kernels, attend_back(): pl.pallas_call(attend_back_kernel, grid=(pairs,), out_shape=[jax.ShapeDty...  34 us
    pallas_call x1, Pallas kernels, attend(): pl.pallas_call(attend_kernel, grid=(pairs,), out_shape=[jax.ShapeDtypeStr...  25 us
    pallas_call x1, Pallas kernels, factors_back(): pl.pallas_call(factors_back_kernel, grid=(seq // BLOCK,), out_shape=[jax....  22.3 us
    pallas_call x1, Pallas kernels, make_factors(): pl.pallas_call(factors_kernel, grid=(seq // BLOCK,), out_shape=[jax.Shape...  13.9 us
    unnamed x38, local copies, waits for them, and re-layouts  10.1 us

profile of v2, /device:TPU:0, one launch (start us, length us, event | category | flops | bytes accessed | tf_op | source)
XLA Modules:
  0.0 489.3 jit_solution(888528850806766462)
XLA Ops:
  0.6 0.8 copy.44
  1.4 0.8 copy.45
  2.1 1.5 concatenate.3.refs_0_
  3.6 1.7 copy.46.doc_col
  5.4 113.7 %gather_weights.1 = (bf16[2,2,4,2,32,896]{5,4,3,2,1,0:T(8,128)(2,1)}, bf16[2,2,4,2,32,1024]{5,4,3,2,1,0:T(8,128)(2,1)}, bf16[2,2,4,2,32,2816]{5,4,3,2,1,0:T(8,12...) custom-call(bf16[32,896]{1,0:T(8,128)(2,1)} %concatenate.3.refs_0_, ...), custom_call_target="tpu_custom_call" | custom-call | tf_op jit(solution)/shard_map/gather_weights/pallas_call | solution.py:491
  119.1 2.0 convert_reduce_fusion
  121.1 13.9 %factors.1 = (bf16[1024,1024]{1,0:T(8,128)(2,1)}, f32[1024,896]{1,0:T(8,128)}, bf16[1024,1024]{1,0:T(8,128)(2,1)}, bf16[1024,1024]{1,0:T(8,128)(2,1)}, bf16[1024,1024]{1,0:T(8,128)(2,1)}) custom-call(bf16[1024,1024]{1,0:T(8,128)(2,1)} %bitcast.65, f32[1,1024]{1,0:T(1,128)} %bitcast.73, bf16[1024,896]{1,0:T(8,128)(2,1)} %bitcast.63, ...), custom_call_target="tpu_custom_call" | custom-call | tf_op jit(solution)/shard_map/factors/pallas_call | solution.py:115
  135.0 25.0 %attend.1 = (bf16[1024,1024]{1,0:T(8,128)(2,1)}, f32[8,2,1024]{2,1,0:T(2,128)}) custom-call(s32[1024,1]{1,0:T(8,128)} %copy.46.doc_col, s32[1,1024]{1,0:T(1,128)} %doc_row.3, bf16[1024,1024]{1,0:T(8,128)(2,1)} %get-tuple-element.38.query, bf16[1024,1024]{1,0:T(8,128)(2,1)} %get-tuple-element.39.key, bf16[1024,1024]{1,0:T(8,128)(2,1)} %get-tuple-element.40.value), custom_call_target="tpu_custom_call" | custom-call | tf_op jit(solution)/shard_map/attend/pallas_call | solution.py:168
  160.0 0.0 copy-done.8
  160.0 0.0 slice-start.1
  160.1 4.2 multiply_reduce_fusion.2
  164.3 2.0 copy-done
  166.2 0.4 multiply_convert_fusion.1
  166.7 0.0 slice-done
  166.7 0.0 slice-done.1
  166.7 0.0 slice-start.3
  166.7 8.8 %fusion.14 = f32[1024,2816]{1,0:T(8,128)} fusion(bf16[1024,1024]{1,0:T(8,128)(2,1)S(1)} %multiply_convert_fusion.1, bf16[1024,2816]{1,0:T(8,128)(2,1)S(1)} %bitcast.80), kind=kOutput, calls=%fused_computation.41 | convolution fusion | flops 5905580032 | bytes 19398656 | tf_op jit(solution)/shard_map/dot_general | solution.py:28
  175.5 0.0 slice-done.2
  175.6 8.9 %fusion.13 = f32[1024,2816]{1,0:T(8,128)} fusion(bf16[1024,1024]{1,0:T(8,128)(2,1)S(1)} %multiply_convert_fusion.1, bf16[1024,2816]{1,0:T(8,128)(2,1)S(1)} %bitcast.84), kind=kOutput, calls=%fused_computation.40 | convolution fusion | flops 5905580032 | bytes 19398656 | tf_op jit(solution)/shard_map/dot_general | solution.py:28
  184.4 21.9 %fusion.3 = (bf16[1024,2816]{1,0:T(8,128)(2,1)}, bf16[1024,2816]{1,0:T(8,128)(2,1)}, bf16[1024,2816]{1,0:T(8,128)(2,1)}) fusion(f32[1024,2816]{1,0:T(8,128)} %fusion.13, f32[1024,2816]{1,0:T(8,128)} %fusion.14, bf16[2816,1024]{1,0:T(8,128)(2,1)} %bitcast.85, bf16[1,1024,1024]{2,1,0:T(8,128)(2,1)} %param.32), kind=kOutput, calls=%fused_computation.5 | convolution fusion | flops 5948833792 | bytes 48234496 | tf_op jit(solution)/shard_map/dot_general | solution.py:28
  206.4 11.5 %fusion.5 = bf16[1,1024,1024]{2,1,0:T(8,128)(2,1)} fusion(f32[1024,1024]{1,0:T(8,128)} %copy-done, bf16[1024,2816]{1,0:T(8,128)(2,1)} %get-tuple-element.68, bf16[2816,1024]{1,0:T(8,128)(2,1)} %bitcast.86), kind=kOutput, calls=%fused_computation.19 | convolution fusion | flops 5907677184 | bytes 17825792 | tf_op jit(solution)/shard_map/dot_general | solution.py:28
  217.9 9.7 %fusion.15 = f32[1024,1024]{1,0:T(8,128)} fusion(bf16[1024,2816]{1,0:T(8,128)(2,1)S(1)} %copy-done.11, bf16[1024,2816]{1,0:T(8,128)(2,1)} %bitcast.81), kind=kOutput, calls=%fused_computation.42 | convolution fusion | flops 5905580032 | bytes 15728640 | tf_op jit(solution)/shard_map/dot_general | solution.py:28
  227.6 0.0 copy-done.1
  227.6 9.6 %multiply_reduce_fusion = (bf16[1024]{0:T(1024)(128)(2,1)S(1)}, f32[1024]{0:T(1024)S(1)}, f32[1024,1024]{1,0:T(8,128)S(1)}) fusion(f32[1024,1024]{1,0:T(8,128)S(1)} %copy-done.1, f32[1024]{0:T(1024)S(1)} %get-tuple-element.74, f32[1024]{0:T(1024)S(1)} %get-tuple-element.62, f32[1024,1024]{1,0:T(8,128)} %fusion.15, bf16[1024,2816]{1,0:T(8,128)(2,1)S(1)} %copy-done.12, ...), kind=kOutput, calls=%fused_computation.12 | convolution fusion | flops 5912918016 | bytes 24131584 | tf_op jit(solution)/shard_map/dot_general | solution.py:28
  237.2 8.6 %convolution_convert_fusion.1 = bf16[1024,2816]{1,0:T(8,128)(2,1)} fusion(bf16[1024,1024]{1,0:T(8,128)(2,1)S(1)} %multiply_convert_fusion.1, bf16[1024,2816]{1,0:T(8,128)(2,1)S(1)} %copy-done.12), kind=kOutput, calls=%fused_computation.10 | convolution fusion | flops 5908463616 | bytes 13631488 | tf_op jit(solution)/shard_map/dot_general | solution.py:28
  245.8 8.4 %convolution_convert_fusion.2 = bf16[1024,2816]{1,0:T(8,128)(2,1)} fusion(bf16[1024,1024]{1,0:T(8,128)(2,1)S(1)} %multiply_convert_fusion.1, bf16[1024,2816]{1,0:T(8,128)(2,1)S(1)} %copy-done.11), kind=kOutput, calls=%fused_computation.11 | convolution fusion | flops 5908463616 | bytes 13631488 | tf_op jit(solution)/shard_map/dot_general | solution.py:28
  254.2 1.3 multiply_subtract_fusion.g_middle
  255.5 12.4 %convolution_convert_fusion = bf16[2816,1024]{1,0:T(8,128)(2,1)} fusion(bf16[1024,2816]{1,0:T(8,128)(2,1)} %get-tuple-element.68, bf16[1,1024,1024]{2,1,0:T(8,128)(2,1)S(1)} %copy-done.4), kind=kOutput, calls=%fused_computation.9 | convolution fusion | flops 5908463616 | bytes 13631488 | tf_op jit(solution)/shard_map/dot_general | solution.py:28
  267.9 3.8 convolution_convert_fusion.3
  271.7 0.0 copy-done.2
  271.7 3.7 convolution_convert_fusion.4.grad
  275.5 34.0 %attend_back.1 = (f32[1024,1024]{1,0:T(8,128)}, f32[1024,1024]{1,0:T(8,128)}, f32[1024,1024]{1,0:T(8,128)}) custom-call(s32[1024,1]{1,0:T(8,128)} %copy.46.doc_col, s32[1,1024]{1,0:T(1,128)} %doc_row.3, bf16[1024,1024]{1,0:T(8,128)(2,1)} %get-tuple-element.38.query, bf16[1024,1024]{1,0:T(8,128)(2,1)} %get-tuple-element.39.key, ...), custom_call_target="tpu_custom_call" | custom-call | tf_op jit(solution)/shard_map/attend_back/pallas_call | solution.py:210
  309.5 22.3 %factors_back.1 = (bf16[1024,896]{1,0:T(8,128)(2,1)}, bf16[1024,1024]{1,0:T(8,128)(2,1)}, f32[1,1024]{1,0:T(1,128)}) custom-call(bf16[1024,1024]{1,0:T(8,128)(2,1)} %bitcast.66, f32[1,1024]{1,0:T(1,128)} %bitcast.74, bf16[1024,896]{1,0:T(8,128)(2,1)} %bitcast.64, f32[1024,128]{1,0:T(8,128)} %constant.22.clone.cosine, f32[1024,128]{1,0:T(8,128)} %constant.23.clone.sine, ...), custom_call_target="tpu_custom_call" | custom-call | tf_op jit(solution)/shard_map/factors_back/pallas_call | solution.py:272
  331.8 0.0 copy-start.6
  331.8 3.9 convolution_convert_fusion.5
  335.8 0.2 copy.50
  336.0 1.8 dynamic_update_slice.3
  337.8 1.3 copy-done.5
  339.1 136.0 %scatter_gradients.1 = (f32[32,2816]{1,0:T(8,128)}, f32[32,2816]{1,0:T(8,128)}, f32[88,1024]{1,0:T(8,128)}, f32[32,1024]{1,0:T(8,128)}, f32[32,896]{1,0:T(8,128)}) custom-call(bf16[2,2,4,2,32,2816]{5,4,3,2,1,0:T(8,128)(2,1)} %bitcast.68, bf16[2,2,4,2,32,2816]{5,4,3,2,1,0:T(8,128)(2,1)} %bitcast.67, bf16[2,2,4,2,88,1024]{5,4,3,2,1,0:T(8,128)(2,1)} %bitcast.69, ...), custom_call_target="tpu_custom_call" | custom-call | tf_op jit(solution)/shard_map/scatter_gradients/pallas_call | solution.py:698
  475.1 1.5 slice_reduce_fusion
  476.6 1.3 slice.33
  477.9 1.3 fusion.11
  479.3 1.4 fusion.12
  480.7 1.4 slice.34
  482.1 1.6 copy.58
  483.7 1.7 copy.59
  485.4 1.7 copy.60
  487.2 1.7 copy.61
  (31 shorter events, 0.1 us)
Async XLA Ops:
  135.0 25.1 %copy-start.3 = (bf16[1,1024,1024]{2,1,0:T(8,128)(2,1)S(1)}, bf16[1,1024,1024]{2,1,0:T(8,128)(2,1)}, u32[]{:S(2)}) copy-start(bf16[1,1024,1024]{2,1,0:T(8,128)(2,1)} %param.18) | copy-start | bytes 6291460
  135.0 25.1 %copy-start.8 = (bf16[2,2,4,2,32,1024]{5,4,3,2,1,0:T(8,128)(2,1)S(1)}, bf16[2,2,4,2,32,1024]{5,4,3,2,1,0:T(8,128)(2,1)}, u32[]{:S(2)}) copy-start(bf16[2,2,4,2,32,1024]{5,4,3,2,1,0:T(8,128)(2,1)} %get-tuple-element.42) | copy-start | bytes 6291460
  160.0 6.6 %slice-start = ((s8[5767168]{0:T(1024)(128)(4,1)}), s8[4194304]{0:T(1024)(128)(4,1)S(1)}, s32[]{:S(2)}) async-start(s8[5767168]{0:T(1024)(128)(4,1)} %bitcast.78), calls=%async_computation | async-start | bytes 8388608
  160.0 6.6 %slice-start.1 = ((s8[5767168]{0:T(1024)(128)(4,1)}), s8[1572864]{0:T(1024)(128)(4,1)S(1)}, s32[]{:S(2)}) async-start(s8[5767168]{0:T(1024)(128)(4,1)} %bitcast.78), calls=%async_computation.1 | async-start | bytes 3145728
  164.3 2.0 copy-start
  166.2 9.3 %slice-start.2 = ((s8[5767168]{0:T(1024)(128)(4,1)}), s8[4194304]{0:T(1024)(128)(4,1)S(1)}, s32[]{:S(2)}) async-start(s8[5767168]{0:T(1024)(128)(4,1)} %bitcast.82), calls=%async_computation.2 | async-start | bytes 8388608
  166.7 8.9 %slice-start.3 = ((s8[5767168]{0:T(1024)(128)(4,1)}), s8[1572864]{0:T(1024)(128)(4,1)S(1)}, s32[]{:S(2)}) async-start(s8[5767168]{0:T(1024)(128)(4,1)} %bitcast.82), calls=%async_computation.3 | async-start | bytes 3145728
  206.4 11.6 %copy-start.11 = (bf16[1024,2816]{1,0:T(8,128)(2,1)S(1)}, bf16[1024,2816]{1,0:T(8,128)(2,1)}, u32[]{:S(2)}) copy-start(bf16[1024,2816]{1,0:T(8,128)(2,1)} %get-tuple-element.67) | copy-start | bytes 17301508
  217.9 9.7 %copy-start.1 = (f32[1024,1024]{1,0:T(8,128)S(1)}, f32[1024,1024]{1,0:T(8,128)}, u32[]{:S(2)}) copy-start(f32[1024,1024]{1,0:T(8,128)} %copy-done) | copy-start | bytes 12582916
  217.9 9.7 %copy-start.12 = (bf16[1024,2816]{1,0:T(8,128)(2,1)S(1)}, bf16[1024,2816]{1,0:T(8,128)(2,1)}, u32[]{:S(2)}) copy-start(bf16[1024,2816]{1,0:T(8,128)(2,1)} %get-tuple-element.66) | copy-start | bytes 17301508
  245.8 8.4 %copy-start.4 = (bf16[1,1024,1024]{2,1,0:T(8,128)(2,1)S(1)}, bf16[1,1024,1024]{2,1,0:T(8,128)(2,1)}, u32[]{:S(2)}) copy-start(bf16[1,1024,1024]{2,1,0:T(8,128)(2,1)} %param.32) | copy-start | bytes 6291460
  255.5 16.2 %copy-start.2 = (f32[1024,1024]{1,0:T(8,128)}, f32[1024,1024]{1,0:T(8,128)S(1)}, u32[]{:S(2)}) copy-start(f32[1024,1024]{1,0:T(8,128)S(1)} %multiply_subtract_fusion.g_middle) | copy-start | bytes 12582916
  255.5 12.4 %copy-start.10 = (bf16[1024,1024]{1,0:T(8,128)(2,1)S(1)}, bf16[1024,1024]{1,0:T(8,128)(2,1)}, u32[]{:S(2)}) copy-start(bf16[1024,1024]{1,0:T(8,128)(2,1)} %get-tuple-element.41) | copy-start | bytes 6291460
  267.9 3.8 copy-start.9
  309.5 22.3 %copy-start.7 = (bf16[1024,1024]{1,0:T(8,128)(2,1)S(1)}, bf16[1024,1024]{1,0:T(8,128)(2,1)}, u32[]{:S(2)}) copy-start(bf16[1024,1024]{1,0:T(8,128)(2,1)} %get-tuple-element.52) | copy-start | bytes 6291460
  331.8 4.0 copy-start.6
  337.8 1.3 copy-start.5

commit v3 on v2

--- a/solution.py
+++ b/solution.py
@@ -501,9 +501,10 @@
 
 
 class Scatter:
-    def __init__(self, place, src, out, bufs, sems, i):
+    def __init__(self, place, held, out, bufs, sems, i, src=None):
         self.p, self.src, self.out, self.i = place, src, out, i
-        self.own, self.from_core, self.from_a, self.from_b, self.from_z = bufs
+        self.own, self.away = (held, None) if src is not None else (held.at[place.c], held.at[place.at("c", 1)])
+        self.from_core, self.from_a, self.from_b, self.from_z = bufs
         self.local, self.cs, self.cr, self.as_, self.ar, self.bs, self.br, self.zs, self.zr = sems
 
     @staticmethod
@@ -514,11 +515,11 @@
         return [dma((n, nx))] * 3 + [dma((n, m))] * 4 + [dma((n, max(1, nz - 1)))] * 2
 
     @staticmethod
-    def buf_shapes(dims, block):
+    def buf_shapes(dims, block, lead=()):
         ny, nc, nz, nx = dims
         m = max(nx, ny, 2)
-        buf = lambda *s: pltpu.VMEM(s + block, jnp.bfloat16)
-        return [buf(ny, nx, nz), buf(ny, nx, nz), buf(m - 1, m, nz), buf(m - 1, nz), buf(max(1, nz - 1))]
+        buf = lambda *s: pltpu.VMEM(lead + s + block, jnp.bfloat16)
+        return [buf(ny, nx, nz), buf(m - 1, m, nz), buf(m - 1, nz), buf(max(1, nz - 1))]
 
     def copy(self, src, dst, send, recv, axis, k):
         return pltpu.make_async_remote_copy(
@@ -528,12 +529,17 @@
 
     def loads(self):
         p, i = self.p, self.i
+        if self.src is None:
+            return
         for x in range(p.dims[3]):
             yield lambda x=x: pltpu.make_async_copy(self.src.at[:, p.c, :, x], self.own.at[:, x], self.local.at[i, x])
 
     def core_copies(self):
         p, i = self.p, self.i
         if p.dims[1] == 1:
+            return
+        if self.src is None:
+            yield lambda: self.copy(self.away, self.from_core, self.cs.at[i, 0], self.cr.at[i, 0], "c", 1)
             return
         for x in range(p.dims[3]):
             yield lambda x=x: self.copy(
@@ -575,11 +581,14 @@
         pl.when(self.p.c == 1)(lambda: body("x"))
 
     @staticmethod
-    def add(total, terms):
-        value = total[...].astype(jnp.float32)
-        for term in terms:
-            value = value + term[...].astype(jnp.float32)
-        return value
+    def add(into, terms):
+        if len(terms) == 1:
+            into[...] = into[...] + terms[0][...]
+        elif terms:
+            value = into[...].astype(jnp.float32)
+            for term in terms:
+                value = value + term[...].astype(jnp.float32)
+            into[...] = value.astype(jnp.bfloat16)
 
     def start(self):
         for copy in self.core_copies():
@@ -595,11 +604,10 @@
         for copy in self.core_copies():
             copy().wait_recv()
         if nc > 1:
-            def body(t, carry):
-                at = (lax.div(t, nx * nz), lax.rem(lax.div(t, nz), nx), lax.rem(t, nz))
-                self.own[at] = self.add(self.own.at[at], [self.from_core.at[at]]).astype(jnp.bfloat16)
+            def body(y, carry):
+                self.add(self.own.at[y], [self.from_core.at[y]])
                 return carry
-            lax.fori_loop(0, ny * nx * nz, body, 0)
+            lax.fori_loop(0, ny, body, 0)
 
         def go(first):
             for copy in self.a_copies(first):
@@ -615,14 +623,11 @@
                 copy().wait_recv()
             n = ny if first == "y" else nx
 
-            def body(t, carry):
-                j, z = lax.div(t, nz), lax.rem(t, nz)
-                at = (p.y, j, z) if first == "y" else (j, p.x, z)
-                terms = [self.from_a.at[k, j, z] for k in range(n - 1)]
-                self.own[at] = self.add(self.own.at[at], terms).astype(jnp.bfloat16)
+            def body(j, carry):
+                at = (p.y, j) if first == "y" else (j, p.x)
+                self.add(self.own.at[at], [self.from_a.at[k, j] for k in range(n - 1)])
                 return carry
-            if n > 1:
-                lax.fori_loop(0, (nx if first == "y" else ny) * nz, body, 0)
+            lax.fori_loop(0, nx if first == "y" else ny, body, 0)
             for copy in self.b_copies(first):
                 copy().start()
         self.by_core(go)
@@ -636,13 +641,7 @@
                 copy().wait_recv()
             n = nx if first == "y" else ny
 
-            def body(z, carry):
-                at = (p.y, p.x, z)
-                terms = [self.from_b.at[k, z] for k in range(n - 1)]
-                self.own[at] = self.add(self.own.at[at], terms).astype(jnp.bfloat16)
-                return carry
-            if n > 1:
-                lax.fori_loop(0, nz, body, 0)
+            self.add(self.own.at[p.y, p.x], [self.from_b.at[k] for k in range(n - 1)])
         self.by_core(go)
         for copy in self.z_copies():
             copy().start()
@@ -651,8 +650,10 @@
         p = self.p
         for copy in self.z_copies():
             copy().wait_recv()
-        terms = [self.from_z.at[k] for k in range(p.dims[2] - 1)]
-        self.out[...] = self.add(self.own.at[p.y, p.x, p.z], terms)
+        value = self.own[p.y, p.x, p.z].astype(jnp.float32)
+        for k in range(p.dims[2] - 1):
+            value = value + self.from_z[k].astype(jnp.float32)
+        self.out[...] = value
 
     def finish(self):
         for copy in self.core_copies():
@@ -684,7 +685,9 @@
     src, out, rest = refs[:n], refs[n:2 * n], refs[2 * n:]
     bufs, sems = rest[:5 * n], rest[5 * n:]
     enter(place)
-    run_stages([Scatter(place, src[i], out[i], bufs[5 * i:5 * i + 5], sems, i).stages() for i in range(n)])
+    run_stages([
+        Scatter(place, bufs[5 * i], out[i], bufs[5 * i + 1:5 * i + 5], sems, i, src[i]).stages() for i in range(n)
+    ])
 
 
 def scatter(dims, arrays, collective_id):
@@ -693,8 +696,9 @@
     blocks = [(a.shape[0] // devices,) + a.shape[1:] for a in arrays]
     shaped = [a.reshape(dims + b) for a, b in zip(arrays, blocks)]
     scratch = []
+    ny, nc, nz, nx = dims
     for b in blocks:
-        scratch += Scatter.buf_shapes(dims, b)
+        scratch += [pltpu.VMEM((ny, nx, nz) + b, jnp.bfloat16)] + Scatter.buf_shapes(dims, b)
     return pl.pallas_call(
         functools.partial(scatter_kernel, dims, n),
         out_shape=[jax.ShapeDtypeStruct(b, jnp.float32) for b in blocks],
@@ -705,6 +709,197 @@
             collective_id=collective_id, has_side_effects=True, vmem_limit_bytes=56 << 20),
         name="scatter_gradients",
     )(*shaped)
+
+
+READY = 3
+CHUNK = 256
+SLOTS = 4
+TOKENS = 512
+
+
+def mlp_kernel(dims, chunks, ready, *refs):
+    (middle, normed, cot, gain, down, early, local_gu, output, g_middle, g_gain, g_gate_up, g_down, gathered,
+     normed_t, total, inner_s, grads_s, weights, held, from_core, from_a, from_b, from_z, load) = refs[:24]
+    sems = refs[24:]
+    ng = len(Gather.sem_shapes(dims, 1))
+    place = Place(dims)
+    j = pl.program_id(0)
+    seq = normed.shape[0]
+    block = local_gu.shape[1]
+    ny, nc, nz, nx = dims
+
+    def gather_at(m):
+        return Gather(place, local_gu.at[m], gathered.at[m - ready], sems[:ng], m - ready)
+
+    def scatter_at(m):
+        bufs = [b.at[m] for b in (from_core, from_a, from_b, from_z)]
+        return Scatter(place, held.at[lax.rem(m, SLOTS)], g_gate_up.at[m], bufs, sems[ng:], m)
+
+    def do(m, first, body):
+        if isinstance(m, int):
+            if first <= m < chunks:
+                body(m)
+            return
+        pl.when((m >= first) & (m < chunks))(lambda: body(m))
+
+    def fetch(m, slot, start):
+        def go(src):
+            copy = pltpu.make_async_copy(src, weights.at[slot], load.at[slot])
+            copy.start() if start else copy.wait()
+        if start:
+            pl.when(m < ready)(lambda: go(early.at[jnp.minimum(m, ready - 1)]))
+            pl.when((m >= ready) & (m < chunks))(lambda: go(gathered.at[jnp.clip(m - ready, 0, chunks - ready - 1)]))
+        else:
+            go(early.at[0])
+
+    def tick_a(j):
+        do(j + 4, ready + 2, lambda m: gather_at(m).start())
+        do(j + 1, ready, lambda m: gather_at(m).after_second())
+        do(j + 2, ready, lambda m: gather_at(m).after_first())
+        do(j - 3, 0, lambda m: scatter_at(m).after_b())
+
+    def tick_b(j):
+        do(j - 1, 0, lambda m: scatter_at(m).after_core())
+        do(j + 3, ready, lambda m: gather_at(m).after_z())
+        do(j - 2, 0, lambda m: scatter_at(m).after_a())
+        do(j + 1, ready, lambda m: gather_at(m).finish())
+
+    def tick_c(j):
+        do(j, 0, lambda m: scatter_at(m).start())
+        do(j - 3, 0, lambda m: scatter_at(m).after_z())
+        do(j - 3, 0, lambda m: scatter_at(m).finish())
+
+    @pl.when(j == 0)
+    def _():
+        fetch(0, 0, True)
+        enter(place)
+        for m in range(ready, min(ready + 2, chunks)):
+            gather_at(m).start()
+        normed_t[...] = normed[...].T
+
+    slot = lax.rem(j, 2)
+    fetch(j, slot, False)
+    w = weights.at[slot]
+    weight = lambda: w[...].reshape(D, -1)
+
+    def tokens_part(t):
+        r = slice(t * TOKENS, (t + 1) * TOKENS)
+        both = dot(normed[r, :], weight())
+        gate, up = both[:, :CHUNK], both[:, CHUNK:]
+        sig = jax.nn.sigmoid(gate)
+        silu = gate * sig
+        inner = (silu * up).astype(bf16)
+        inner_s[r, :] = inner
+        g_inner = dot(cot[r, :], down[...], NT)
+        g_gate = (g_inner * up * sig * (1.0 + gate * (1.0 - sig))).astype(bf16)
+        grads = jnp.concatenate([g_gate, (g_inner * silu).astype(bf16)], axis=1)
+        grads_s[r, :] = grads
+        out, back = dot(inner, down[...]), dot(grads, weight(), NT)
+
+        @pl.when(j == 0)
+        def _():
+            total[r, :] = out
+            g_middle[r, :] = back
+
+        @pl.when(j > 0)
+        def _():
+            total[r, :] += out
+            g_middle[r, :] += back
+
+    parts = seq // TOKENS
+    tick_a(j)
+    for t in range(parts):
+        tokens_part(t)
+        if t == parts // 2 - 1 or parts == 1:
+            tick_b(j)
+            fetch(j + 1, 1 - slot, True)
+    g_weights = dot(normed_t[...], grads_s[...]).astype(bf16)
+    at = held.at[lax.rem(j, SLOTS)]
+    for y in range(ny):
+        for c in range(nc):
+            for z in range(nz):
+                for x in range(nx):
+                    row = (((y * nc + c) * nz + z) * nx + x) * block
+                    at[c, y, x, z] = g_weights[row:row + block]
+    tick_c(j)
+    g_down[...] = dot(inner_s[...], cot[...], TN).astype(bf16)
+
+    @pl.when(j == chunks - 1)
+    def _():
+        for t in range(seq // 256):
+            r = slice(t * 256, t * 256 + 256)
+            m = middle[r, :]
+            s = rms(m)
+            output[r, :] = (m + total[r, :]).astype(bf16)
+            g_normed = g_middle[r, :]
+            u = g_normed * gain[...]
+            g_middle[r, :] = cot[r, :].astype(f32) + s * u - m * (s * s * s * jnp.mean(u * m, axis=-1, keepdims=True))
+            part = jnp.sum(g_normed * m * s, axis=0, keepdims=True)
+            if t == 0:
+                g_gain[...] = part
+            else:
+                g_gain[...] += part
+        for k in range(3):
+            tick_a(chunks + k)
+            tick_b(chunks + k)
+            tick_c(chunks + k)
+
+
+def mlp(dims, middle, normed, cot, gain, down, early, local_gu, collective_id):
+    chunks, block, width = local_gu.shape
+    ready = early.shape[0]
+    seq = normed.shape[0]
+    ny, nc, nz, nx = dims
+    whole = lambda *s: pl.BlockSpec(s, lambda i: (0,) * len(s))
+    vmem = lambda s, t: pltpu.VMEM(s, t)
+    return pl.pallas_call(
+        functools.partial(mlp_kernel, dims, chunks, ready),
+        grid=(chunks,),
+        out_shape=[
+            jax.ShapeDtypeStruct((seq, D), bf16),
+            jax.ShapeDtypeStruct((seq, D), f32),
+            jax.ShapeDtypeStruct((1, D), f32),
+            jax.ShapeDtypeStruct((chunks, block, width), f32),
+            jax.ShapeDtypeStruct((chunks * CHUNK, D), bf16),
+            jax.ShapeDtypeStruct((chunks - ready,) + dims + (block, width), bf16),
+        ],
+        in_specs=[whole(seq, D), whole(seq, D), whole(seq, D), whole(1, D), pl.BlockSpec((CHUNK, D), lambda i: (i, 0)), ANY, ANY],
+        out_specs=[whole(seq, D), whole(seq, D), whole(1, D), whole(chunks, block, width),
+                   pl.BlockSpec((CHUNK, D), lambda i: (i, 0)), ANY],
+        scratch_shapes=[
+            vmem((D, seq), bf16), vmem((seq, D), f32), vmem((seq, CHUNK), bf16), vmem((seq, width), bf16),
+            vmem((2,) + dims + (block, width), bf16), vmem((SLOTS, nc, ny, nx, nz, block, width), bf16),
+        ] + Scatter.buf_shapes(dims, (block, width), (chunks,)) + [pltpu.SemaphoreType.DMA((2,))]
+        + Gather.sem_shapes(dims, chunks - ready) + Scatter.sem_shapes(dims, chunks),
+        compiler_params=pltpu.CompilerParams(
+            collective_id=collective_id, has_side_effects=True, vmem_limit_bytes=62 << 20),
+        name="mlp",
+    )(middle, normed, cot, gain, down, early, local_gu)
+
+
+def plain_mlp(middle, normed_two, cotangent, gain, gate_w, up_w, down_w):
+    gate, up = dot(normed_two, gate_w), dot(normed_two, up_w)
+    sig = jax.nn.sigmoid(gate)
+    silu = gate * sig
+    inner = (silu * up).astype(bf16)
+    output = (middle + dot(inner, down_w)).astype(bf16)
+    grad_inner = dot(cotangent, down_w, NT)
+    grad_gate = (grad_inner * up * sig * (1.0 + gate * (1.0 - sig))).astype(bf16)
+    grad_up = (grad_inner * silu).astype(bf16)
+    grad_normed = dot(grad_gate, gate_w, NT) + dot(grad_up, up_w, NT)
+    scale = rms(middle)
+    gained = grad_normed * gain
+    grad_middle = (
+        cotangent.astype(f32)
+        + scale * gained
+        - middle * scale**3 * jnp.mean(gained * middle, axis=-1, keepdims=True)
+    )
+    grad_gain = jnp.sum(grad_normed * middle * scale, axis=0, keepdims=True)
+    outer_sum = lambda left, right: dot(left, right, TN).astype(bf16)
+    return (
+        output, grad_middle, grad_gain,
+        outer_sum(inner, cotangent), outer_sum(normed_two, grad_gate), outer_sum(normed_two, grad_up),
+    )
 
 
 def on_device(
@@ -738,9 +933,19 @@
         + (jnp.zeros((norm_gain.shape[0], PACKED - gains_at - 2), bf16),),
         axis=1,
     )
-    packed_w, output_w, gate_w, up_w, down_w = gather(
-        dims, [packed, w_output, w_gate, w_up, w_down], 0
-    )
+    block = w_gate.shape[0]
+    fused = block % 16 == 0 and w_gate.shape[1] % CHUNK == 0 and seq_len % TOKENS == 0
+    if fused:
+        chunked = lambda w: w.reshape(block, -1, CHUNK).transpose(1, 0, 2)
+        gate_up = jnp.concatenate([chunked(w_gate), chunked(w_up)], axis=2)
+        packed_w, output_w, down_w, *early = gather(
+            dims, [packed, w_output, w_down] + [gate_up[i] for i in range(READY)], 0
+        )
+        early = jnp.stack(early).reshape((READY,) + dims + gate_up.shape[1:])
+    else:
+        packed_w, output_w, gate_w, up_w, down_w = gather(
+            dims, [packed, w_output, w_gate, w_up, w_down], 0
+        )
     gain_one, gain_two = [packed_w[:, gains_at + i].astype(f32).reshape(1, D) for i in (0, 1)]
 
     inputs = tokens.reshape(seq_len, D)
@@ -748,29 +953,19 @@
     normed, factors, query, key, value = make_factors(inputs, gain_one, packed_w, tables)
     mixed, lse = attend(doc_col, doc_row, query, key, value)
 
+    outer_sum = lambda left, right: dot(left, right, TN).astype(bf16)
     middle = inputs.astype(f32) + dot(mixed, output_w)
-    scale_two = rms(middle)
-    normed_two = (middle * scale_two * gain_two).astype(bf16)
-    gate_proj, up_proj = dot(normed_two, gate_w), dot(normed_two, up_w)
-    sigmoid_gate = jax.nn.sigmoid(gate_proj)
-    silu_gate = gate_proj * sigmoid_gate
-    inner_act = (silu_gate * up_proj).astype(bf16)
-    output = (middle + dot(inner_act, down_w)).astype(bf16)
-
+    normed_two = (middle * rms(middle) * gain_two).astype(bf16)
     cotangent = out_grad.reshape(seq_len, D)
-    grad_inner = dot(cotangent, down_w, NT)
-    grad_gate = (
-        grad_inner * up_proj * sigmoid_gate * (1.0 + gate_proj * (1.0 - sigmoid_gate))
-    ).astype(bf16)
-    grad_up = (grad_inner * silu_gate).astype(bf16)
-    grad_normed_two = dot(grad_gate, gate_w, NT) + dot(grad_up, up_w, NT)
-    gained_two = grad_normed_two * gain_two
-    grad_mlp_gain = jnp.sum(grad_normed_two * middle * scale_two, axis=0)
-    grad_middle = (
-        cotangent.astype(f32)
-        + scale_two * gained_two
-        - middle * scale_two**3 * jnp.mean(gained_two * middle, axis=-1, keepdims=True)
-    )
+    if fused:
+        output, grad_middle, grad_mlp_gain, gate_up_out, grad_down, _ = mlp(
+            dims, middle, normed_two, cotangent, gain_two, down_w, early, gate_up, 1
+        )
+        mlp_grads = [grad_down]
+    else:
+        output, grad_middle, grad_mlp_gain, *mlp_grads = plain_mlp(
+            middle, normed_two, cotangent, gain_two, gate_w, up_w, down_w
+        )
     grad_branch = grad_middle.astype(bf16)
     grad_mixed = dot(grad_branch, output_w, NT).astype(bf16)
 
@@ -780,20 +975,15 @@
     grad_factors, grad_tokens, grad_norm_gain = factors_back(
         inputs, gain_one, packed_w, tables, factors, grad_query, grad_key, grad_value, grad_middle
     )
-    outer_sum = lambda left, right: dot(left, right, TN).astype(bf16)
-    gains = jnp.stack([grad_norm_gain[0], grad_mlp_gain], axis=1).astype(bf16)
+    gains = jnp.stack([grad_norm_gain[0], grad_mlp_gain[0]], axis=1).astype(bf16)
     packed_grad = lax.dynamic_update_slice(outer_sum(normed, grad_factors), gains, (0, gains_at))
-    gate_out, up_out, down_out, output_out, packed_out = scatter(
-        dims,
-        [
-            outer_sum(normed_two, grad_gate),
-            outer_sum(normed_two, grad_up),
-            outer_sum(inner_act, cotangent),
-            outer_sum(mixed, grad_branch),
-            packed_grad,
-        ],
-        1,
+    *mlp_out, output_out, packed_out = scatter(
+        dims, mlp_grads + [outer_sum(mixed, grad_branch), packed_grad], 2
     )
+    if fused:
+        whole = lambda g: g.transpose(1, 0, 2).reshape(block, -1)
+        mlp_out += [whole(gate_up_out[:, :, :CHUNK]), whole(gate_up_out[:, :, CHUNK:])]
+    down_out, gate_out, up_out = mlp_out
     dims_and_heads = [packed_out[:, lo:hi] for lo, hi in zip(edges, edges[1:])]
     grads = [g for pair in zip(dims_and_heads[3:], dims_and_heads[:3]) for g in pair]
     return (

time: 499 us -> 435 us (0.87)
  matrix products: 115 us -> 18.5 us
  Pallas kernels: 345 us -> 376 us
  other arithmetic: 3.78 us -> 9.04 us
    pallas_call x0 -> x1, Pallas kernels: none -> 128 us  [mlp(): pl.pallas_call(functools.partial(mlp_kernel, dims, chunks, ready), grid=(...]
    dot_general x13 -> x4, matrix products: 115 us -> 18.5 us  [dot(): return lax.dot_general(a, b, dims, preferred_element_type=f32)]
    pallas_call x1, Pallas kernels: 136 us -> 71.4 us  [scatter(): pl.pallas_call(functools.partial(scatter_kernel, dims, n), out_shape=[jax...]
    pallas_call x1, Pallas kernels: 114 us -> 81.8 us  [gather(): pl.pallas_call(functools.partial(gather_kernel, dims, n), out_shape=[jax....]
    unnamed x38 -> x34, local copies, waits for them, and re-layouts: 10.1 us -> 6.09 us
where the time goes in v3:
time: 435 us; the launch traced here: 427 us
  Pallas kernels  376 us (86%)
  local copies, waits for them, and re-layouts  21.7 us (5%)
  matrix products  18.5 us (4%)
  other arithmetic  9.04 us (2%)
    pallas_call x1, Pallas kernels, mlp(): pl.pallas_call(functools.partial(mlp_kernel, dims, chunks, ready), grid=(...  128 us
    pallas_call x1, Pallas kernels, gather(): pl.pallas_call(functools.partial(gather_kernel, dims, n), out_shape=[jax....  81.8 us
    pallas_call x1, Pallas kernels, scatter(): pl.pallas_call(functools.partial(scatter_kernel, dims, n), out_shape=[jax...  71.4 us
    pallas_call x1, Pallas kernels, attend_back(): pl.pallas_call(attend_back_kernel, grid=(pairs,), out_shape=[jax.ShapeDty...  33.9 us
    pallas_call x1, Pallas kernels, attend(): pl.pallas_call(attend_kernel, grid=(pairs,), out_shape=[jax.ShapeDtypeStr...  25 us
    pallas_call x1, Pallas kernels, factors_back(): pl.pallas_call(factors_back_kernel, grid=(seq // BLOCK,), out_shape=[jax....  22.3 us
    dot_general x4, matrix products, dot(): return lax.dot_general(a, b, dims, preferred_element_type=f32)  18.5 us
    pallas_call x1, Pallas kernels, make_factors(): pl.pallas_call(factors_kernel, grid=(seq // BLOCK,), out_shape=[jax.Shape...  13.9 us

profile of v3, /device:TPU:0, one launch (start us, length us, event | category | flops | bytes accessed | tf_op | source)
XLA Modules:
  0.0 426.9 jit_solution(4570338923757837628)
XLA Ops:
  0.6 0.0 copy-start.8
  0.7 0.8 copy.46
  1.4 0.8 copy.47
  2.2 1.5 concatenate.7.refs_0_
  3.7 1.0 bitcast_bitcast_fusion
  4.7 0.6 fusion.5
  5.3 0.8 pad_maximum_fusion.1.refs_6_
  6.1 0.0 copy-done.8
  6.1 1.0 copy.50.doc_col
  7.2 81.8 %gather_weights.1 = (bf16[2,2,4,2,32,896]{5,4,3,2,1,0:T(8,128)(2,1)}, bf16[2,2,4,2,32,1024]{5,4,3,2,1,0:T(8,128)(2,1)}, bf16[2,2,4,2,88,1024]{5,4,3,2,1,0:T(8,12...) custom-call(bf16[32,896]{1,0:T(8,128)(2,1)} %concatenate.7.refs_0_, ...), custom_call_target="tpu_custom_call" | custom-call | tf_op jit(solution)/shard_map/gather_weights/pallas_call | solution.py:491
  89.0 2.0 convert_reduce_fusion
  91.0 3.8 pad_maximum_fusion.refs_5_
  94.8 13.9 %factors.1 = (bf16[1024,1024]{1,0:T(8,128)(2,1)}, f32[1024,896]{1,0:T(8,128)}, bf16[1024,1024]{1,0:T(8,128)(2,1)}, bf16[1024,1024]{1,0:T(8,128)(2,1)}, bf16[1024,1024]{1,0:T(8,128)(2,1)}) custom-call(bf16[1024,1024]{1,0:T(8,128)(2,1)} %bitcast.56, f32[1,1024]{1,0:T(1,128)} %bitcast.73, bf16[1024,896]{1,0:T(8,128)(2,1)} %bitcast.54, ...), custom_call_target="tpu_custom_call" | custom-call | tf_op jit(solution)/shard_map/factors/pallas_call | solution.py:115
  108.7 25.0 %attend.1 = (bf16[1024,1024]{1,0:T(8,128)(2,1)}, f32[8,2,1024]{2,1,0:T(2,128)}) custom-call(s32[1024,1]{1,0:T(8,128)} %copy.50.doc_col, s32[1,1024]{1,0:T(1,128)} %doc_row.3, bf16[1024,1024]{1,0:T(8,128)(2,1)} %get-tuple-element.42.query, bf16[1024,1024]{1,0:T(8,128)(2,1)} %get-tuple-element.43.key, bf16[1024,1024]{1,0:T(8,128)(2,1)} %get-tuple-element.44.value), custom_call_target="tpu_custom_call" | custom-call | tf_op jit(solution)/shard_map/attend/pallas_call | solution.py:168
  133.8 0.0 copy-done.1
  133.8 0.0 copy-done.13
  133.8 4.1 multiply_reduce_fusion
  137.9 0.0 copy-done.9
  137.9 2.0 copy-done
  140.0 1.8 multiply_convert_fusion.refs_1_
  141.7 127.9 %mlp.1 = (bf16[1024,1024]{1,0:T(8,128)(2,1)}, f32[1024,1024]{1,0:T(8,128)}, f32[1,1024]{1,0:T(1,128)}, f32[11,32,512]{2,1,0:T(8,128)}, bf16[2816,1024]{1,0:T(8,1...) custom-call(f32[1024,1024]{1,0:T(8,128)} %copy-done, bf16[1024,1024]{1,0:T(8,128)(2,1)} %multiply_convert_fusion.refs_1_, ...), custom_call_target="tpu_custom_call" | custom-call | tf_op jit(solution)/shard_map/mlp/pallas_call | solution.py:855
  269.6 6.7 %convolution_convert_fusion = bf16[1024,1024]{1,0:T(8,128)(2,1)} fusion(bf16[1024,1024]{1,0:T(8,128)(2,1)} %get-tuple-element.45, f32[1024,1024]{1,0:T(8,128)} %get-tuple-element.53.g_middle), kind=kOutput, calls=%fused_computation.4 | convolution fusion | flops 2149580800 | bytes 8388608 | tf_op jit(solution)/shard_map/dot_general | solution.py:28
  276.3 0.0 copy-done.2
  276.3 0.0 copy-start.5
  276.3 3.8 convolution_convert_fusion.1.grad
  280.1 0.0 copy-done.10
  280.1 0.1 slice_bitcast_fusion
  280.2 0.8 copy.60
  281.0 0.8 copy.59
  281.7 33.9 %attend_back.1 = (f32[1024,1024]{1,0:T(8,128)}, f32[1024,1024]{1,0:T(8,128)}, f32[1024,1024]{1,0:T(8,128)}) custom-call(s32[1024,1]{1,0:T(8,128)} %copy.50.doc_col, s32[1,1024]{1,0:T(1,128)} %doc_row.3, bf16[1024,1024]{1,0:T(8,128)(2,1)} %get-tuple-element.42.query, bf16[1024,1024]{1,0:T(8,128)(2,1)} %get-tuple-element.43.key, ...), custom_call_target="tpu_custom_call" | custom-call | tf_op jit(solution)/shard_map/attend_back/pallas_call | solution.py:210
  315.6 22.3 %factors_back.1 = (bf16[1024,896]{1,0:T(8,128)(2,1)}, bf16[1024,1024]{1,0:T(8,128)(2,1)}, f32[1,1024]{1,0:T(1,128)}) custom-call(bf16[1024,1024]{1,0:T(8,128)(2,1)} %bitcast.57, f32[1,1024]{1,0:T(1,128)} %bitcast.74, bf16[1024,896]{1,0:T(8,128)(2,1)} %bitcast.55, f32[1024,128]{1,0:T(8,128)} %constant.19.clone.cosine, f32[1024,128]{1,0:T(8,128)} %constant.20.clone.sine, ...), custom_call_target="tpu_custom_call" | custom-call | tf_op jit(solution)/shard_map/factors_back/pallas_call | solution.py:272
  338.0 0.0 copy-done.12
  338.0 0.0 copy-start.11
  338.0 3.9 convolution_convert_fusion.2
  341.9 0.0 copy-done.11
  342.0 0.2 copy.53
  342.2 1.8 dynamic_update_slice.3
  344.0 0.0 copy-start.4
  344.0 1.2 copy-done.4
  345.2 71.4 %scatter_gradients.1 = (f32[88,1024]{1,0:T(8,128)}, f32[32,1024]{1,0:T(8,128)}, f32[32,896]{1,0:T(8,128)}) custom-call(bf16[2,2,4,2,88,1024]{5,4,3,2,1,0:T(8,128)(2,1)} %bitcast.59, bf16[2,2,4,2,32,1024]{5,4,3,2,1,0:T(8,128)(2,1)} %bitcast.61, bf16[2,2,4,2,32,896]{5,4,3,2,1,0:T(8,128)(2,1)} %bitcast.63), custom_call_target="tpu_custom_call" | custom-call | tf_op jit(solution)/shard_map/scatter_gradients/pallas_call | solution.py:702
  416.7 1.5 slice_reduce_fusion
  418.2 1.3 slice.51
  419.5 1.3 fusion.8
  420.9 1.4 fusion.9
  422.3 1.4 slice.52
  423.7 1.3 copy.67
  425.0 0.7 copy.68
  425.7 0.7 copy.69
  (21 shorter events, 0.1 us)
Async XLA Ops:
  0.6 5.5 %copy-start.8 = (s32[1,1024]{1,0:T(1,128)S(1)}, s32[1,1024]{1,0:T(1,128)}, u32[]{:S(2)}) copy-start(s32[1,1024]{1,0:T(1,128)} %doc_row.3) | copy-start | bytes 12292
  91.0 46.9 %copy-start.9 = (f32[1024]{0:T(1024)}, f32[1024]{0:T(1024)S(1)}, u32[]{:S(2)}) copy-start(f32[1024]{0:T(1024)S(1)} %get-tuple-element.68) | copy-start | bytes 12292
  108.7 25.0 %copy-start.1 = (bf16[1,1024,1024]{2,1,0:T(8,128)(2,1)S(1)}, bf16[1,1024,1024]{2,1,0:T(8,128)(2,1)}, u32[]{:S(2)}) copy-start(bf16[1,1024,1024]{2,1,0:T(8,128)(2,1)} %param.18) | copy-start | bytes 6291460
  108.7 25.0 %copy-start.13 = (bf16[2,2,4,2,32,1024]{5,4,3,2,1,0:T(8,128)(2,1)S(1)}, bf16[2,2,4,2,32,1024]{5,4,3,2,1,0:T(8,128)(2,1)}, u32[]{:S(2)}) copy-start(bf16[2,2,4,2,32,1024]{5,4,3,2,1,0:T(8,128)(2,1)} %get-tuple-element.46) | copy-start | bytes 6291460
  137.9 2.1 copy-start
  269.6 6.7 %copy-start.2 = (f32[1024,1024]{1,0:T(8,128)S(1)}, f32[1024,1024]{1,0:T(8,128)}, u32[]{:S(2)}) copy-start(f32[1024,1024]{1,0:T(8,128)} %get-tuple-element.53.g_middle) | copy-start | bytes 12582916
  269.6 6.7 %copy-start.14 = (bf16[2,2,4,2,32,1024]{5,4,3,2,1,0:T(8,128)(2,1)S(1)}, bf16[2,2,4,2,32,1024]{5,4,3,2,1,0:T(8,128)(2,1)}, u32[]{:S(2)}) copy-start(bf16[2,2,4,2,32,1024]{5,4,3,2,1,0:T(8,128)(2,1)} %get-tuple-element.46) | copy-start | bytes 6291460
  276.3 3.8 copy-start.10
  276.3 3.8 copy-start.5
  315.6 22.3 %copy-start.12 = (bf16[1024,1024]{1,0:T(8,128)(2,1)S(1)}, bf16[1024,1024]{1,0:T(8,128)(2,1)}, u32[]{:S(2)}) copy-start(bf16[1024,1024]{1,0:T(8,128)(2,1)} %get-tuple-element.60) | copy-start | bytes 6291460
  338.0 3.9 copy-start.11
  344.0 1.2 copy-start.4
  345.2 78.5 %copy-start.3 = (bf16[1024,1024]{1,0:T(8,128)(2,1)S(1)}, bf16[1024,1024]{1,0:T(8,128)(2,1)}, u32[]{:S(2)}) copy-start(bf16[1024,1024]{1,0:T(8,128)(2,1)} %get-tuple-element.51) | copy-start | bytes 6291460
  423.7 1.3 copy-start.7
  423.7 2.0 copy-start.6
